TPU v7x, 128 devices: a whole 4x4x4 slice. The times are simulated.
128 devices in a mesh: front: 4 (over x), row: 4 (over z), col: 8 (over y, core).
Axes of the slice: x: 4, y: 4, z: 4, core: 2. Of those that a mesh axis runs over, the one named last changes fastest.
Arguments:
- tiles: float32 [4096, 256, 256], P(('front', 'row', 'col')), may hold values from -6 to 6
- dest: int32 [4096, 1], P(('front', 'row', 'col')), may hold values from 0 to 15; in each aligned block of 32 rows (0 to 31, 32 to 63, ...) at most 4 rows name the same one
- block_row: int32 [4096], P(('front', 'row', 'col')), may hold values from 0 to 9
- block_col: int32 [4096], P(('front', 'row', 'col')), may hold values from 0 to 4
- rows_from: int32 [4096, 256], P(('front', 'row', 'col')), may hold values from 0 to 255, each once within a row
- cols_from: int32 [4096, 256], P(('front', 'row', 'col')), may hold values from 0 to 255, each once within a row
- initial: float32 [4, 10240, 512], P('front', 'row', 'col'), may hold values from -6 to 60, as said below
- pattern: int32 [4, 2, 40], P('front'), may hold values 0 or 1
Outputs:
- factored: float32 [4, 10240, 10240], P('front', 'row', 'col')
Inputs may be any that keep to these rules, and one draw needn't show every extreme that they name: `dest`: in the rows of one device no destination is named by more than 4 tiles, a bound that some block reaches. `rows_from`: each row is a permutation. `cols_from`: each row is a permutation. `initial`: the first 512 rows form a symmetric block whose diagonal entries exceed the sum of magnitudes of the other entries in their rows.
All inputs are finite; a program needn't handle non-finite values. No bound on the sum of `pattern` on one device may be relied on, other than what follows from the above.
Results may differ from a plain program's by a relative error of at most 0.0001.
Values sent between devices are 32-bit elements; how exact they have to be, the bound alone decides.
No kernel may reach another device: no remote copies, remote signals or barrier semaphores. Data moves between devices by JAX's collectives and lax.ppermute only.
A program may use at most 192 MiB of HBM per device.

v0:
```python
import jax
import jax.numpy as jnp
from jax import lax
from jax.sharding import PartitionSpec as P

ORDER = 10240
BS = 256
NPANEL = 2
CAP = 4
PIV = 512


HIGH = lax.Precision.HIGHEST


def from_root(block, axis, owner):
    block = jnp.where(lax.axis_index(axis) == owner, block, jnp.zeros_like(block))
    return lax.psum(block, axis)


def lower_sym(block):
    return jnp.tril(block) + jnp.tril(block, -1).T


def body(tiles, dest, block_row, block_col, rows_from, cols_from, initial, pattern):
    n_front = lax.axis_size("front")
    n_row = lax.axis_size("row")
    n_col = lax.axis_size("col")
    my_row = lax.axis_index("row")
    my_col = lax.axis_index("col")
    row_span = ORDER // n_row
    col_span = ORDER // n_col
    row_blocks = row_span // BS
    col_blocks = col_span // BS
    lead = PIV // BS
    targets = n_front * n_row
    slots = targets * CAP
    moved = jnp.take_along_axis(tiles, rows_from[:, :, None], axis=1)
    moved = jnp.take_along_axis(moved, cols_from[:, None, :], axis=2)
    target = dest[:, 0]
    owner_row = target % n_row
    local_row = jnp.where(owner_row == 0, lead + block_row % (row_blocks - lead), block_row)
    block_id = local_row * col_blocks + block_col
    same = (target[:, None] == target[None, :]).astype(jnp.int32)
    earlier = jnp.sum(jnp.tril(same, -1), axis=1)
    slot = target * CAP + earlier
    choose = jnp.arange(slots, dtype=jnp.int32)[:, None] == slot[None, :]
    outgoing = jnp.einsum("st,tij->sij", choose.astype(jnp.float32), moved, precision=HIGH)
    labels = jnp.where(
        jnp.any(choose, axis=1), jnp.sum(jnp.where(choose, block_id[None, :], 0), axis=1), -1
    )
    incoming, names = (
        lax.all_to_all(outgoing, ("front", "row"), split_axis=0, concat_axis=0, tiled=True),
        lax.all_to_all(labels, ("front", "row"), split_axis=0, concat_axis=0, tiled=True),
    )
    count = row_blocks * col_blocks
    owners = (jnp.arange(count, dtype=jnp.int32)[:, None] == names[None, :]).astype(jnp.float32)
    blocks = jnp.einsum("bs,sij->bij", owners, incoming, precision=HIGH)
    grid = (
        blocks.reshape(row_blocks, col_blocks, BS, BS)
        .transpose(0, 2, 1, 3)
        .reshape(row_span, col_span)
    )
    columns = lax.all_gather(initial[0], "col", axis=1, tiled=True)
    first = my_col == 0
    grid = grid.at[:, :PIV].add(jnp.where(first, columns, jnp.zeros_like(columns)))
    glob_row = my_row * row_span + jnp.arange(row_span, dtype=jnp.int32)
    glob_col = my_col * col_span + jnp.arange(col_span, dtype=jnp.int32)
    identity = jnp.eye(BS, dtype=jnp.float32)
    slab = grid[:, 0:BS]
    for panel in range(NPANEL):
        low = panel * BS
        corner = from_root(slab[low : low + BS], "row", 0)
        factor = jnp.linalg.cholesky(jnp.where(first, lower_sym(corner), identity))
        solved = lax.linalg.triangular_solve(
            factor, slab, left_side=False, lower=True, transpose_a=True
        )
        local_flags = lax.dynamic_slice_in_dim(pattern[0, panel], my_row * row_blocks, row_blocks)
        flags = jnp.repeat(local_flags, BS)
        keep = (glob_row >= low + BS) & (flags == 1)
        rows = jnp.where(keep[:, None], solved, jnp.zeros_like(solved))
        top_owner = my_row == 0
        column = rows.at[low : low + BS].set(jnp.where(top_owner, factor, rows[low : low + BS]))
        spread = from_root(rows, "col", 0)
        every = lax.all_gather(spread, "row", axis=0, tiled=True)
        across = lax.dynamic_slice_in_dim(every, my_col * col_span, col_span, 0)
        ahead = low + BS
        grid = grid - jnp.dot(spread, across.T, precision=HIGH)
        grid = grid.at[:, low : low + BS].set(jnp.where(first, column, grid[:, low : low + BS]))
        if panel + 1 < NPANEL:
            slab = grid[:, ahead : ahead + BS]
    upper = (glob_row[:, None] < PIV) & (glob_col[None, :] >= PIV)
    grid = jnp.where(upper, jnp.zeros_like(grid), grid)
    return grid[None]


def solution(mesh):
    placed = (
        P(("front", "row", "col"), None, None),
        P(("front", "row", "col"), None),
        P(("front", "row", "col")),
        P(("front", "row", "col")),
        P(("front", "row", "col"), None),
        P(("front", "row", "col"), None),
        P("front", "row", "col"),
        P("front", None, None),
    )
    return jax.shard_map(
        body, mesh=mesh, in_specs=placed, out_specs=P("front", "row", "col"), check_vma=False
    )
```

profile of v0, /device:TPU:7, one launch (start us, length us, event | category | flops | bytes accessed | tf_op | source)
XLA Modules:
  0.0 1398.7 jit_solution(6061388510909078777)
XLA Ops:
  19.9 137.7 %gather_fusion = f32[8192,256]{1,0:T(8,128)} fusion(f32[32,256,256]{2,1,0:T(8,128)} %param.21, s32[8192]{0:T(1024)S(1)} %bitcast.119), kind=kCustom, calls=%fused_computation | custom fusion | bytes 16842752 | tf_op jit(solution)/shard_map/jit(take_along_axis)/gather | solution.py:38
  174.7 137.3 %gather_fusion.1 = f32[8192,256]{1,0:T(8,128)} fusion(f32[32,256,256]{1,2,0:T(8,128)} %broadcast_select_fusion, s32[8192]{0:T(1024)S(1)} %bitcast.118), kind=kCustom, calls=%fused_computation.1 | custom fusion | bytes 16842752 | tf_op jit(solution)/shard_map/jit(take_along_axis)/gather | solution.py:39
  325.7 12.9 fusion.2
  338.6 19.3 %copy.91 = f32[64,256,256]{2,1,0:T(8,128)} copy(f32[64,256,256]{2,0,1:T(8,128)S(1)} %fusion.2) | data formatting | bytes 33554432 | tf_op jit(solution)/shard_map/st,tij->sij/dot_general | solution.py:48
  367.6 274.3 %all-to-all-done.1 = f32[64,256,256]{2,1,0:T(8,128)} async-done(((f32[64,256,256]{2,1,0:T(8,128)}), f32[64,256,256]{2,1,0:T(8,128)}, u32[]{:S(2)}, u32[]{:S(2)}) %all-to-all-start.1) | async-done | bytes 16777248 | tf_op jit(solution)/shard_map/all_to_all | solution.py:53
  641.8 26.0 %fusion = f32[50,256,256]{2,0,1:T(8,128)} fusion(f32[64,256,256]{2,1,0:T(8,128)} %all-to-all-done.1, s32[64]{0:T(128)S(1)} %eq.100), kind=kOutput, calls=%fused_computation.6 | convolution fusion | flops 2516585472 | bytes 29884672 | tf_op jit(solution)/shard_map/bs,sij->bij/dot_general | solution.py:58
  667.8 14.3 %copy.93 = f32[50,256,256]{2,1,0:T(8,128)} copy(f32[50,256,256]{2,0,1:T(8,128)} %fusion) | data formatting | bytes 26214400 | tf_op jit(solution)/shard_map/bs,sij->bij/dot_general | solution.py:58
  682.1 18.4 %copy.122 = f32[10,256,5,256]{1,0,3,2:T(8,128)} copy(f32[10,256,5,256]{3,1,2,0:T(8,128)} %bitcast.122) | data formatting | bytes 26214400 | tf_op jit(solution)/shard_map/reshape | solution.py:62
  700.5 18.7 %copy.134 = f32[160,8,10,256]{3,1,2,0:T(8,128)} copy(f32[160,8,10,256]{3,2,1,0:T(8,128)} %bitcast.121) | data formatting | bytes 26214400
  729.7 63.5 %all-reduce.6.cloned.1.call-done = f32[256,256]{0,1:T(8,128)} async-done(((f32[256,256]{0,1:T(8,128)}), f32[256,256]{0,1:T(8,128)}) %all-reduce.6.cloned.1.call-update) | async-done | bytes 262160 | tf_op jit(solution)/shard_map/psum | solution.py:18
  795.6 11.7 cholesky.130
  817.6 11.7 cholesky.147
  836.5 19.7 %custom-call.18 = f32[2,128,128]{1,2,0:T(8,128)S(1)} custom-call(f32[2,128,128]{2,1,0:T(8,128)S(1)} %get-tuple-element.81), custom_call_target="InvertDiagBlocksLowerTriangular" | custom-call | tf_op jit(solution)/shard_map/triangular_solve/custom-call.0 | solution.py:75
  865.7 68.0 %all-reduce.8.cloned.1.call-done = f32[2560,256]{0,1:T(8,128)} async-done(((f32[2560,256]{0,1:T(8,128)}), f32[2560,256]{0,1:T(8,128)}) %all-reduce.8.cloned.1.call-update) | async-done | bytes 2621456 | tf_op jit(solution)/shard_map/psum | solution.py:18
  936.3 101.6 %all-gather.5.cloned.1.call-done = f32[10240,256]{0,1:T(8,128)} async-done(((f32[2560,256]{0,1:T(8,128)}), f32[10240,256]{0,1:T(8,128)}) %all-gather.5.cloned.1.call-update) | async-done | bytes 10485776 | tf_op jit(solution)/shard_map/all_gather | solution.py:85
  1037.9 15.5 %convolution_subtract_fusion.1 = f32[2560,1280]{0,1:T(8,128)S(1)} fusion(f32[2560,1280]{0,1:T(8,128)} %get-tuple-element.135, f32[2560,256]{0,1:T(8,128)S(1)} %copy-done.1, f32[10240,256]{0,1:T(8,128)} %all-gather.5.cloned.1.call-done, s32[]{:T(128)S(6)} %select_n.175), kind=kOutput, calls=%fused_computation.9 | convolution fusion | flops 10069606400 | bytes 30146564 | tf_op jit(solution)/shard_map/dot_general | solution.py:88
  1060.9 40.7 %all-reduce.10.cloned.1.call-done = f32[256,256]{0,1:T(8,128)} async-done(((f32[256,256]{0,1:T(8,128)}), f32[256,256]{0,1:T(8,128)}) %all-reduce.10.cloned.1.call-update) | async-done | bytes 262160 | tf_op jit(solution)/shard_map/psum | solution.py:18
  1103.9 11.7 cholesky.164
  1125.9 11.7 cholesky.181
  1145.2 19.7 %custom-call.20 = f32[2,128,128]{1,2,0:T(8,128)S(1)} custom-call(f32[2,128,128]{2,1,0:T(8,128)S(1)} %get-tuple-element.82), custom_call_target="InvertDiagBlocksLowerTriangular" | custom-call | tf_op jit(solution)/shard_map/triangular_solve/custom-call.0 | solution.py:75
  1174.5 68.0 %all-reduce.12.cloned.1.call-done = f32[2560,256]{0,1:T(8,128)} async-done(((f32[2560,256]{0,1:T(8,128)}), f32[2560,256]{0,1:T(8,128)}) %all-reduce.12.cloned.1.call-update) | async-done | bytes 2621456 | tf_op jit(solution)/shard_map/psum | solution.py:18
  1245.0 101.6 %all-gather.7.cloned.1.call-done = f32[10240,256]{0,1:T(8,128)} async-done(((f32[2560,256]{0,1:T(8,128)}), f32[10240,256]{0,1:T(8,128)}) %all-gather.7.cloned.1.call-update) | async-done | bytes 10485776 | tf_op jit(solution)/shard_map/all_gather | solution.py:85
  1346.6 16.1 %convolution_subtract_fusion = f32[2560,1280]{0,1:T(8,128)} fusion(f32[2560,1280]{0,1:T(8,128)} %copy-done, f32[2560,256]{0,1:T(8,128)S(1)} %copy-done.2, f32[10240,256]{0,1:T(8,128)} %all-gather.7.cloned.1.call-done, s32[]{:T(128)S(6)} %select_n.175), kind=kOutput, calls=%fused_computation.8 | convolution fusion | flops 10069606400 | bytes 30146564 | tf_op jit(solution)/shard_map/dot_general | solution.py:88
  1377.8 13.9 copy.117
  (145 shorter events, 156.4 us)
Async XLA Ops:
  9.0 348.9 %all-to-all-start = ((s32[16,4,1]{1,2,0:T(1,128)}), s32[16,4,1]{1,2,0:T(1,128)S(1)}, u32[]{:S(2)}, u32[]{:S(2)}) async-start(s32[16,4,1]{1,2,0:T(1,128)} %bitcast.1), calls=%async_computation | async-start | bytes 16384 | tf_op jit(solution)/shard_map/all_to_all | solution.py:54
  357.9 8.3 copy-start.6
  357.9 283.9 %all-to-all-start.1 = ((f32[64,256,256]{2,1,0:T(8,128)}), f32[64,256,256]{2,1,0:T(8,128)}, u32[]{:S(2)}, u32[]{:S(2)}) async-start(f32[64,256,256]{2,1,0:T(8,128)} %copy.91), calls=%async_computation.1 | async-start | bytes 33554432 | tf_op jit(solution)/shard_map/all_to_all | solution.py:53
  364.7 354.5 %all-gather.9.cloned.1.call-start = ((), (), s32[]{:S(2)}) async-start(), calls=%async_computation.8 | async-start | bytes 5898240 | tf_op jit(solution)/shard_map/all_gather | solution.py:64
  365.5 427.8 %all-reduce.6.cloned.1.call-start = ((), (), s32[]{:S(2)}) async-start(), calls=%async_computation.2 | async-start | bytes 524288 | tf_op jit(solution)/shard_map/psum | solution.py:18
  726.3 2.3 copy-start.3
  729.3 204.4 %all-reduce.8.cloned.1.call-start = ((), (), s32[]{:S(2)}) async-start(), calls=%async_computation.3 | async-start | bytes 5242880 | tf_op jit(solution)/shard_map/psum | solution.py:18
  865.7 172.2 %all-gather.5.cloned.1.call-start = ((), (), s32[]{:S(2)}) async-start(), calls=%async_computation.4 | async-start | bytes 13107200 | tf_op jit(solution)/shard_map/all_gather | solution.py:85
  933.8 104.1 %copy-start.1 = (f32[2560,256]{0,1:T(8,128)S(1)}, f32[2560,256]{0,1:T(8,128)}, u32[]{:S(2)}) copy-start(f32[2560,256]{0,1:T(8,128)} %all-reduce.8.cloned.1.call-done) | copy-start | bytes 7864324
  933.8 167.7 %all-reduce.10.cloned.1.call-start = ((), (), s32[]{:S(2)}) async-start(), calls=%async_computation.5 | async-start | bytes 524288 | tf_op jit(solution)/shard_map/psum | solution.py:18
  1037.9 15.5 %copy-start.4 = (f32[2560,256]{0,1:T(8,128)S(1)}, f32[2560,256]{0,1:T(8,128)}, u32[]{:S(2)}) copy-start(f32[2560,256]{0,1:T(8,128)} %fusion.13) | copy-start | bytes 7864324
  1054.8 5.0 copy-start
  1060.5 182.0 %all-reduce.12.cloned.1.call-start = ((), (), s32[]{:S(2)}) async-start(), calls=%async_computation.6 | async-start | bytes 5242880 | tf_op jit(solution)/shard_map/psum | solution.py:18
  1174.4 172.2 %all-gather.7.cloned.1.call-start = ((), (), s32[]{:S(2)}) async-start(), calls=%async_computation.7 | async-start | bytes 13107200 | tf_op jit(solution)/shard_map/all_gather | solution.py:85
  1242.5 104.1 %copy-start.2 = (f32[2560,256]{0,1:T(8,128)S(1)}, f32[2560,256]{0,1:T(8,128)}, u32[]{:S(2)}) copy-start(f32[2560,256]{0,1:T(8,128)} %all-reduce.12.cloned.1.call-done) | copy-start | bytes 7864324
  1346.6 16.1 %copy-start.5 = (f32[2560,256]{0,1:T(8,128)S(1)}, f32[2560,256]{0,1:T(8,128)}, u32[]{:S(2)}) copy-start(f32[2560,256]{0,1:T(8,128)} %fusion.12) | copy-start | bytes 7864324
Sparse Core Ops, SparseCore 0:
  367.2 39.3 all-gather.8
  729.5 63.7 all-reduce.5
  865.8 67.9 all-reduce.7
  935.4 102.4 all-gather.4
  1060.6 40.8 all-reduce.9
  1174.5 67.9 all-reduce.11
  1244.1 102.4 all-gather.6
where the time goes:
time: 1410 us; the launch traced here: 1400 us
  waiting for transfers between devices  719 us (51%)
  local copies, waits for them, and re-layouts  398 us (28%)
  other arithmetic  165 us (12%)
  matrix products  84.4 us (6%)
  between operations  16.7 us (1%)
  starting transfers between devices  15.2 us (1%)
    all_to_all x1, waiting for transfers between devices, body(): lax.all_to_all(outgoing, ('front', 'row'), split_axis=0, concat_axis=0, t...  274 us
    psum x4, waiting for transfers between devices, from_root(): return lax.psum(block, axis)  240 us
    all_gather x2, waiting for transfers between devices, body(): every = lax.all_gather(spread, 'row', axis=0, tiled=True)  203 us
    gather x2, local copies, waits for them, and re-layouts, body(): moved = jnp.take_along_axis(tiles, rows_from[:, :, None], axis=1)  147 us
    gather x2, local copies, waits for them, and re-layouts, body(): moved = jnp.take_along_axis(moved, cols_from[:, None, :], axis=2)  146 us
    another operation x13, other arithmetic, body(): factor = jnp.linalg.cholesky(jnp.where(first, lower_sym(corner), identity))  68.7 us
    another operation x5, other arithmetic, body(): lax.linalg.triangular_solve(factor, slab, left_side=False, lower=True, tr...  39.4 us
    dot_general x2, matrix products, body(): grid = grid - jnp.dot(spread, across.T, precision=HIGH)  31.6 us
  transfers between devices with their start and end apart: 9, of which 7 were waited for; matrix products, arithmetic and copies ran while one was open for 30% of the time, Pallas kernels for 0%

commit v1 on v0

v1 whole, which is shorter than its diff:
```python
import jax
import jax.numpy as jnp
from jax import lax
from jax.experimental import pallas as pl
from jax.experimental.pallas import tpu as pltpu
from jax.sharding import PartitionSpec as P

ORDER = 10240
BS = 256
CAP = 4
PIV = 512
STRIPS = (64, 64, 64, 64)
OFFSETS = tuple(sum(STRIPS[:q]) for q in range(len(STRIPS)))
NSTRIP = len(STRIPS)
RING = 8

HIGH = lax.Precision.HIGHEST
f32, bf16, i32 = jnp.float32, jnp.bfloat16, jnp.int32


def lower_sym(block):
    return jnp.tril(block) + jnp.tril(block, -1).T


def permute_kernel(slot_ref, tile_ref, rows_ref, cols_ref, *out_refs):
    tile = tile_ref[0]
    high = tile.astype(bf16)
    rest = tile - high.astype(f32)
    mid = rest.astype(bf16)
    low = (rest - mid.astype(f32)).astype(bf16)
    place = lax.broadcasted_iota(i32, (BS, BS), 0)
    pick_rows = jnp.where(place == rows_ref[0], 1.0, 0.0).astype(bf16)
    pick_cols = jnp.where(place == cols_ref[0], 1.0, 0.0).astype(bf16)
    parts = jnp.concatenate([high, mid, low], axis=1)
    moved = lax.dot_general(
        pick_rows, parts, (((0,), (0,)), ((), ())), preferred_element_type=f32
    ).astype(bf16)
    out = jnp.dot(moved[:, :BS], pick_cols, preferred_element_type=f32)
    out = out + jnp.dot(moved[:, BS : 2 * BS], pick_cols, preferred_element_type=f32)
    out = out + jnp.dot(moved[:, 2 * BS :], pick_cols, preferred_element_type=f32)
    for q, out_ref in enumerate(out_refs):
        out_ref[0] = out[OFFSETS[q] : OFFSETS[q] + STRIPS[q]]


def permute(slot, tiles, rows_from, cols_from, slots):
    count = tiles.shape[0]
    return pl.pallas_call(
        permute_kernel,
        grid_spec=pltpu.PrefetchScalarGridSpec(
            num_scalar_prefetch=1,
            grid=(count,),
            in_specs=[
                pl.BlockSpec((1, BS, BS), lambda t, slot: (t, 0, 0)),
                pl.BlockSpec((1, 1, BS), lambda t, slot: (t, 0, 0)),
                pl.BlockSpec((1, 1, BS), lambda t, slot: (t, 0, 0)),
            ],
            out_specs=[
                pl.BlockSpec((1, h, BS), lambda t, slot: (slot[t], 0, 0)) for h in STRIPS
            ],
        ),
        out_shape=[jax.ShapeDtypeStruct((slots, h, BS), f32) for h in STRIPS],
        compiler_params=pltpu.CompilerParams(vmem_limit_bytes=32 << 20),
        cost_estimate=pl.CostEstimate(
            flops=12 * count * BS**3, bytes_accessed=8 * count * BS * BS, transcendentals=0
        ),
        name="permute_tiles",
    )(slot, tiles, rows_from[:, None, :], cols_from[:, None, :])


def slab_kernel(height, meta, initial_ref, in_ref, out_ref, ring, sems):
    total = meta[128]

    def copy(g):
        return pltpu.make_async_copy(in_ref.at[meta[g]], ring.at[g % RING], sems.at[g % RING])

    for g in range(RING):

        @pl.when(g < total)
        def _():
            copy(g).start()

    out_ref[...] = initial_ref[...]

    @pl.loop(0, total)
    def _(g):
        copy(g).wait()
        spot = meta[64 + g]
        cols = pl.ds(pl.multiple_of((spot % 2) * BS, BS), BS)
        out_ref[spot // 2, :, cols] += ring[g % RING]

        @pl.when(g + RING < total)
        def _():
            copy(g + RING).start()


def slab_strip(meta, initial, incoming, height):
    blocks = initial.shape[0]
    return pl.pallas_call(
        lambda *refs: slab_kernel(height, *refs),
        grid_spec=pltpu.PrefetchScalarGridSpec(
            num_scalar_prefetch=1,
            grid=(1,),
            in_specs=[
                pl.BlockSpec((blocks, height, PIV), lambda i, meta: (0, 0, 0)),
                pl.BlockSpec(memory_space=pl.ANY),
            ],
            out_specs=pl.BlockSpec((blocks, height, PIV), lambda i, meta: (0, 0, 0)),
            scratch_shapes=[
                pltpu.VMEM((RING, height, BS), f32),
                pltpu.SemaphoreType.DMA((RING,)),
            ],
        ),
        out_shape=jax.ShapeDtypeStruct((blocks, height, PIV), f32),
        compiler_params=pltpu.CompilerParams(vmem_limit_bytes=32 << 20),
        cost_estimate=pl.CostEstimate(
            flops=0, bytes_accessed=12 * blocks * height * PIV, transcendentals=0
        ),
        name="slab_strip",
    )(meta, initial, incoming)


def halves(x):
    high = x.astype(bf16)
    return high, (x - high.astype(f32)).astype(bf16)


def nt(a, b):
    return lax.dot_general(a, b, (((1,), (1,)), ((), ())), preferred_element_type=f32)


def final_kernel(col_blocks, *refs):
    meta = refs[0]
    slab = refs[1 : 1 + NSTRIP]
    across = refs[1 + NSTRIP : 1 + 2 * NSTRIP]
    first_inv, second_inv, cross, first_factor, second_factor = refs[1 + 2 * NSTRIP : 6 + 2 * NSTRIP]
    incoming = refs[6 + 2 * NSTRIP : 6 + 3 * NSTRIP]
    out_ref, a_high, a_low, ring, sems = refs[6 + 3 * NSTRIP :]
    b = pl.program_id(0)
    total = meta[138]

    def copies(g):
        return [
            pltpu.make_async_copy(
                incoming[q].at[meta[g]],
                ring.at[g % RING, pl.ds(OFFSETS[q], STRIPS[q])],
                sems.at[g % RING, q],
            )
            for q in range(NSTRIP)
        ]

    def solve(block, keep_first, keep_second):
        one = jnp.dot(block[:, :BS], first_inv[...], precision=HIGH, preferred_element_type=f32)
        one = jnp.where(keep_first == 1, one, 0.0)
        two = jnp.dot(block[:, BS:], second_inv[...], precision=HIGH, preferred_element_type=f32)
        two = two - jnp.dot(one, cross[...], precision=HIGH, preferred_element_type=f32)
        return one, jnp.where(keep_second == 1, two, 0.0)

    @pl.when(b == 0)
    def _():
        for g in range(RING):

            @pl.when(g < total)
            def _():
                for c in copies(g):
                    c.start()

        for cb in range(col_blocks):
            block = jnp.concatenate([ref[cb] for ref in across], axis=0)
            one, two = solve(block, meta[159 + cb], meta[164 + cb])
            high, low = halves(jnp.concatenate([one, two], axis=1))
            a_high[cb * BS : (cb + 1) * BS] = high
            a_low[cb * BS : (cb + 1) * BS] = low

    one, two = solve(
        jnp.concatenate([ref[0] for ref in slab], axis=0), meta[139 + b], meta[149 + b]
    )
    top = meta[169] == 1
    high, low = halves(
        jnp.where(jnp.logical_and(top, b < 2), 0.0, jnp.concatenate([one, two], axis=1))
    )
    for cb in range(col_blocks):
        rows = slice(cb * BS, (cb + 1) * BS)
        product = nt(high, a_high[rows]) + (nt(high, a_low[rows]) + nt(low, a_high[rows]))
        out_ref[:, rows] = -product

    @pl.loop(meta[128 + b], meta[129 + b])
    def _(g):
        for c in copies(g):
            c.wait()
        cols = pl.ds(pl.multiple_of(meta[64 + g] * BS, BS), BS)
        out_ref[:, cols] += ring[g % RING]

        @pl.when(g + RING < total)
        def _():
            for c in copies(g + RING):
                c.start()

    @pl.when(meta[170] == 1)
    def _():
        out_ref[:, :BS] = jnp.where(jnp.logical_and(top, b == 0), first_factor[...], one)
        out_ref[:, BS:PIV] = jnp.where(jnp.logical_and(top, b == 1), second_factor[...], two)


def final(meta, slab, across, mats, incoming, row_blocks, col_blocks):
    whole = pl.BlockSpec((BS, BS), lambda b, meta: (0, 0))
    return pl.pallas_call(
        lambda *refs: final_kernel(col_blocks, *refs),
        grid_spec=pltpu.PrefetchScalarGridSpec(
            num_scalar_prefetch=1,
            grid=(row_blocks,),
            in_specs=[pl.BlockSpec((1, h, PIV), lambda b, meta: (b, 0, 0)) for h in STRIPS]
            + [pl.BlockSpec((col_blocks, h, PIV), lambda b, meta: (0, 0, 0)) for h in STRIPS]
            + [whole] * 5
            + [pl.BlockSpec(memory_space=pl.ANY)] * NSTRIP,
            out_specs=pl.BlockSpec((BS, col_blocks * BS), lambda b, meta: (b, 0)),
            scratch_shapes=[
                pltpu.VMEM((col_blocks * BS, PIV), bf16),
                pltpu.VMEM((col_blocks * BS, PIV), bf16),
                pltpu.VMEM((RING, BS, BS), f32),
                pltpu.SemaphoreType.DMA((RING, NSTRIP)),
            ],
        ),
        out_shape=jax.ShapeDtypeStruct((row_blocks * BS, col_blocks * BS), f32),
        compiler_params=pltpu.CompilerParams(vmem_limit_bytes=48 << 20),
        cost_estimate=pl.CostEstimate(
            flops=6 * row_blocks * col_blocks * BS * BS * PIV,
            bytes_accessed=4 * 2 * row_blocks * col_blocks * BS * BS,
            transcendentals=0,
        ),
        name="place_and_update",
    )(meta, *slab, *across, *mats, *incoming)


def factors(corner, keep):
    first = jnp.linalg.cholesky(lower_sym(corner[:BS, :BS]))
    eye = jnp.eye(BS, dtype=f32)
    first_inv = lax.linalg.triangular_solve(first, eye, left_side=True, lower=True)
    below = jnp.dot(corner[BS:, :BS], first_inv.T, precision=HIGH)
    below = jnp.where(keep, below, jnp.zeros_like(below))
    rest = corner[BS:, BS:] - jnp.dot(below, below.T, precision=HIGH)
    second = jnp.linalg.cholesky(lower_sym(rest))
    second_inv = lax.linalg.triangular_solve(second, eye, left_side=True, lower=True)
    cross = jnp.dot(below.T, second_inv.T, precision=HIGH)
    return first_inv.T, second_inv.T, cross, first, second


def spread_col(x, my_col):
    arrived = [lax.ppermute(x, "col", [(0, to)]) for to in (2, 6, 4)]
    even = jnp.where(my_col == 0, x, arrived[0] + arrived[1] + arrived[2])
    odd = lax.ppermute(even, "col", [(c, c + 1) for c in (0, 2, 4, 6)])
    return jnp.where(my_col % 2 == 0, even, odd)


def spread_row(x, my_row, my_col, n_row, n_col):
    half = x.shape[0] // 2
    own = lax.dynamic_slice_in_dim(x, (my_col % 2) * half, half, 0)
    out = own
    for step in range(1, n_row):
        pairs = [
            ((c // 2) * n_col + c, ((c // 2 + step) % n_row) * n_col + c) for c in range(n_col)
        ]
        got = lax.ppermute(own, ("row", "col"), pairs)
        out = jnp.where((my_row - my_col // 2) % n_row == step, got, out)
    return out


def ordered(key, valid, span):
    count = key.shape[0]
    key = jnp.where(valid, key, span)
    index = jnp.arange(count, dtype=i32)
    ahead = (key[None, :] < key[:, None]) | (
        (key[None, :] == key[:, None]) & (index[None, :] < index[:, None])
    )
    rank = jnp.sum(ahead.astype(i32), axis=1)
    chosen = rank[None, :] == index[:, None]
    order = jnp.sum(jnp.where(chosen, index[None, :], 0), axis=1)
    return order, jnp.sum(jnp.where(chosen, key[None, :], 0), axis=1), key


def body(tiles, dest, block_row, block_col, rows_from, cols_from, initial, pattern):
    n_front = lax.axis_size("front")
    n_row = lax.axis_size("row")
    n_col = lax.axis_size("col")
    my_row = lax.axis_index("row")
    my_col = lax.axis_index("col")
    row_blocks = ORDER // n_row // BS
    col_blocks = ORDER // n_col // BS
    lead = PIV // BS
    slots = n_front * n_row * CAP
    target = dest[:, 0]
    owner_row = target % n_row
    local_row = jnp.where(owner_row == 0, lead + block_row % (row_blocks - lead), block_row)
    block_id = local_row * col_blocks + block_col
    same = (target[:, None] == target[None, :]).astype(i32)
    slot = target * CAP + jnp.sum(jnp.tril(same, -1), axis=1)
    choose = jnp.arange(slots, dtype=i32)[:, None] == slot[None, :]
    labels = jnp.where(
        jnp.any(choose, axis=1), jnp.sum(jnp.where(choose, block_id[None, :], 0), axis=1), -1
    )
    names = lax.all_to_all(labels, ("front", "row"), split_axis=0, concat_axis=0, tiled=True)
    outgoing = permute(slot, tiles, rows_from, cols_from, slots)
    incoming = [
        lax.all_to_all(part, ("front", "row"), split_axis=0, concat_axis=0, tiled=True)
        for part in outgoing
    ]
    valid = names >= 0
    order, sorted_id, key = ordered(names, valid, row_blocks * col_blocks)
    bounds = jnp.arange(row_blocks + 1, dtype=i32)[:, None] * col_blocks
    starts = jnp.sum((key[None, :] < bounds).astype(i32), axis=1)
    in_slab = valid & (names % col_blocks < lead) & (my_col == 0)
    slab_key = (names // col_blocks) * lead + names % col_blocks
    slab_order, slab_id, _ = ordered(slab_key, in_slab, row_blocks * lead)
    slab_meta = jnp.concatenate([slab_order, slab_id, jnp.sum(in_slab.astype(i32))[None]])

    def kept(first_block, count):
        blocks = first_block + jnp.arange(count, dtype=i32)
        flags = lax.dynamic_slice_in_dim(pattern[0], first_block, count, axis=1)
        ahead = blocks[None, :] > jnp.arange(2, dtype=i32)[:, None]
        return jnp.where(ahead, flags, 0).reshape(-1)

    meta = jnp.concatenate(
        [
            order,
            sorted_id % col_blocks,
            starts,
            kept(my_row * row_blocks, row_blocks),
            kept(my_col * col_blocks, col_blocks),
            (my_row == 0).astype(i32)[None],
            (my_col == 0).astype(i32)[None],
        ]
    )

    pivot = jnp.where(my_row == 0, initial[0, :PIV], 0.0)
    corner = lax.all_gather(lax.psum(pivot, "row"), "col", axis=1, tiled=True)
    mats = factors(corner, pattern[0, 0, 1] == 1)
    columns = lax.all_gather(initial[0], "col", axis=1, tiled=True)
    columns = columns.reshape(row_blocks, BS, PIV)

    slab, across = [], []
    for q in range(NSTRIP):
        rows = slice(OFFSETS[q], OFFSETS[q] + STRIPS[q])
        strip = slab_strip(slab_meta, columns[:, rows], incoming[q], STRIPS[q])
        strip = spread_col(strip, my_col)
        slab.append(strip)
        across.append(spread_row(strip, my_row, my_col, n_row, n_col))
    return final(meta, slab, across, mats, incoming, row_blocks, col_blocks)[None]


def solution(mesh):
    placed = (
        P(("front", "row", "col"), None, None),
        P(("front", "row", "col"), None),
        P(("front", "row", "col")),
        P(("front", "row", "col")),
        P(("front", "row", "col"), None),
        P(("front", "row", "col"), None),
        P("front", "row", "col"),
        P("front", None, None),
    )
    return jax.shard_map(
        body, mesh=mesh, in_specs=placed, out_specs=P("front", "row", "col"), check_vma=False
    )
```

time: 1410 us -> 594 us (0.42)
  the two profiles are of different devices: /device:TPU:7 before, /device:TPU:10 now
where the time goes in v1:
time: 594 us; the launch traced here: 586 us
  waiting for transfers between devices  250 us (42%)
  other arithmetic  132 us (22%)
  starting transfers between devices  75.4 us (13%)
  Pallas kernels  64 us (11%)
  local copies, waits for them, and re-layouts  37.4 us (6%)
  between operations  17.7 us (3%)
  matrix products  8.68 us (1%)
    ppermute x12, waiting for transfers between devices, spread_row(): got = lax.ppermute(own, ('row', 'col'), pairs)  91.9 us
    psum x1, waiting for transfers between devices, body(): corner = lax.all_gather(lax.psum(pivot, 'row'), 'col', axis=1, tiled=True)  76.6 us
    all_to_all x4, waiting for transfers between devices, body(): lax.all_to_all(part, ('front', 'row'), split_axis=0, concat_axis=0, tiled...  46 us
    ppermute x12, waiting for transfers between devices, spread_col(): arrived = [lax.ppermute(x, 'col', [(0, to)]) for to in (2, 6, 4)]  34.9 us
    another operation x7, other arithmetic, factors(): second = jnp.linalg.cholesky(lower_sym(rest))  34.7 us
    another operation x6, other arithmetic, factors(): first = jnp.linalg.cholesky(lower_sym(corner[:BS, :BS]))  34 us
    pallas_call x1, Pallas kernels, final(): pl.pallas_call(lambda *refs: final_kernel(col_blocks, *refs), grid_spec=p...  32.3 us
    all_to_all x4, starting transfers between devices, body(): lax.all_to_all(part, ('front', 'row'), split_axis=0, concat_axis=0, tiled...  29.9 us
  transfers between devices with their start and end apart: 36, of which 8 were waited for; matrix products, arithmetic and copies ran while one was open for 28% of the time, Pallas kernels for 5%

profile of v1, /device:TPU:10, one launch (start us, length us, event | category | flops | bytes accessed | tf_op | source)
XLA Modules:
  0.0 585.9 jit_solution(5398022474092289389)
XLA Ops:
  9.0 8.3 %all-to-all-start = ((s32[16,4,1]{1,2,0:T(1,128)}), s32[16,4,1]{1,2,0:T(1,128)S(1)}, u32[]{:S(2)}, u32[]{:S(2)}) async-start(s32[16,4,1]{1,2,0:T(1,128)} %bitcast.1), calls=%async_computation | async-start | bytes 16384 | tf_op jit(solution)/shard_map/all_to_all | solution.py:300
  18.9 25.7 %permute_tiles.1 = (f32[64,64,256]{2,1,0:T(8,128)S(1)}, f32[64,64,256]{2,1,0:T(8,128)S(1)}, f32[64,64,256]{2,1,0:T(8,128)S(1)}, f32[64,64,256]{2,1,0:T(8,128)S(1)}) custom-call(s32[32]{0:T(128)S(1)} %get-tuple-element.76.slot_ref, f32[32,256,256]{2,1,0:T(8,128)} %tile_ref.1, s32[32,1,256]{2,1,0:T(1,128)S(1)} %broadcast_in_dim.137.rows_ref, ...), custom_call_target="tpu_custom_call" | custom-call | flops 6442450944 | bytes 16777216 | tf_op jit(solution)/shard_map/permute_tiles/pallas_call | solution.py:47
  52.6 7.2 %all-to-all-start.2 = ((f32[64,64,256]{2,1,0:T(8,128)}), f32[64,64,256]{2,1,0:T(8,128)}, u32[]{:S(2)}, u32[]{:S(2)}) async-start(f32[64,64,256]{2,1,0:T(8,128)} %copy-done.4), calls=%async_computation.2 | async-start | bytes 8388608 | tf_op jit(solution)/shard_map/all_to_all | solution.py:303
  61.5 76.6 %all-reduce.3.cloned.1.call-done = f32[512,64]{0,1:T(8,128)} async-done(((f32[512,64]{0,1:T(8,128)}), f32[512,64]{0,1:T(8,128)}) %all-reduce.3.cloned.1.call-update) | async-done | bytes 131088 | tf_op jit(solution)/shard_map/psum | solution.py:334
  138.9 6.4 %all-to-all-start.3 = ((f32[64,64,256]{2,1,0:T(8,128)}), f32[64,64,256]{2,1,0:T(8,128)}, u32[]{:S(2)}, u32[]{:S(2)}) async-start(f32[64,64,256]{2,1,0:T(8,128)} %copy-done.3), calls=%async_computation.3 | async-start | bytes 8388608 | tf_op jit(solution)/shard_map/all_to_all | solution.py:303
  148.7 46.0 %all-to-all-done.3.refs_2_.refs_16_ = f32[64,64,256]{2,1,0:T(8,128)} async-done(((f32[64,64,256]{2,1,0:T(8,128)}), f32[64,64,256]{2,1,0:T(8,128)}, u32[]{:S(2)}, u32[]{:S(2)}) %all-to-all-start.3) | async-done | bytes 4194336 | tf_op jit(solution)/shard_map/all_to_all | solution.py:303
  194.8 8.9 %all-to-all-start.4 = ((f32[64,64,256]{2,1,0:T(8,128)}), f32[64,64,256]{2,1,0:T(8,128)}, u32[]{:S(2)}, u32[]{:S(2)}) async-start(f32[64,64,256]{2,1,0:T(8,128)} %copy-done.2), calls=%async_computation.4 | async-start | bytes 8388608 | tf_op jit(solution)/shard_map/all_to_all | solution.py:303
  207.8 11.7 %cholesky.130 = f32[128,128]{1,0:T(8,128)S(1)} custom-call(f32[128,128]{1,0:T(8,128)S(1)} %copy.72), custom_call_target="Cholesky" | custom-call | tf_op jit(solution)/shard_map/jit(cholesky)/cholesky | solution.py:235
  219.5 9.8 %custom-call.13 = f32[1,128,128]{1,2,0:T(8,128)S(1)} custom-call(f32[1,128,128]{2,1,0:T(8,128)S(1)} %get-tuple-element.72), custom_call_target="InvertDiagBlocksLowerTriangular" | custom-call | tf_op jit(solution)/shard_map/jit(cholesky)/cholesky | solution.py:235
  230.0 11.7 %cholesky.147 = f32[128,128]{1,0:T(8,128)S(1)} custom-call(f32[128,128]{1,0:T(8,128)S(1)} %copy.74), custom_call_target="Cholesky" | custom-call | tf_op jit(solution)/shard_map/jit(cholesky)/cholesky | solution.py:235
  247.6 20.1 %custom-call.14 = f32[2,128,128]{1,2,0:T(8,128)S(1)} custom-call(f32[2,128,128]{2,1,0:T(8,128)S(1)} %get-tuple-element.29), custom_call_target="InvertDiagBlocksLowerTriangular" | custom-call | tf_op jit(solution)/shard_map/triangular_solve/custom-call.0 | solution.py:237
  268.5 7.3 %all-to-all-start.1 = ((f32[64,64,256]{2,1,0:T(8,128)}), f32[64,64,256]{2,1,0:T(8,128)}, u32[]{:S(2)}, u32[]{:S(2)}) async-start(f32[64,64,256]{2,1,0:T(8,128)} %copy-done.1), calls=%async_computation.1 | async-start | bytes 8388608 | tf_op jit(solution)/shard_map/all_to_all | solution.py:303
  278.2 5.9 %copy.68 = f32[1,2560,512]{2,1,0:T(8,128)} copy(f32[1,2560,512]{1,2,0:T(8,128)} %all-gather.6.cloned.1.call-done) | data formatting | bytes 10485760 | tf_op jit(solution)/shard_map/all_gather | solution.py:336
  295.9 11.7 %cholesky.164 = f32[128,128]{1,0:T(8,128)S(1)} custom-call(f32[128,128]{1,0:T(8,128)S(1)} %cholesky.197), custom_call_target="Cholesky" | custom-call | tf_op jit(solution)/shard_map/jit(cholesky)/cholesky | solution.py:241
  307.6 9.8 %custom-call.15 = f32[1,128,128]{1,2,0:T(8,128)S(1)} custom-call(f32[1,128,128]{2,1,0:T(8,128)S(1)} %get-tuple-element.68), custom_call_target="InvertDiagBlocksLowerTriangular" | custom-call | tf_op jit(solution)/shard_map/jit(cholesky)/cholesky | solution.py:241
  319.6 11.7 %cholesky.181 = f32[128,128]{1,0:T(8,128)S(1)} custom-call(f32[128,128]{1,0:T(8,128)S(1)} %convolution_subtract_fusion.3), custom_call_target="Cholesky" | custom-call | tf_op jit(solution)/shard_map/jit(cholesky)/cholesky | solution.py:241
  355.2 19.7 %custom-call.16 = f32[2,128,128]{1,2,0:T(8,128)S(1)} custom-call(f32[2,128,128]{2,1,0:T(8,128)S(1)} %get-tuple-element.30), custom_call_target="InvertDiagBlocksLowerTriangular" | custom-call | tf_op jit(solution)/shard_map/triangular_solve/custom-call.0 | solution.py:242
  394.4 12.4 %collective-permute-done.4 = f32[10,64,512]{2,1,0:T(8,128)} collective-permute-done((f32[10,64,512]{2,1,0:T(8,128)}, f32[10,64,512]{2,1,0:T(8,128)}, u32[]{:S(2)}, u32[]{:S(2)}) %collective-permute-start.4) | collective-permute-done | bytes 1310752 | tf_op jit(solution)/shard_map/ppermute | solution.py:248
  412.3 22.5 %collective-permute-done = f32[10,64,512]{2,1,0:T(8,128)} collective-permute-done((f32[10,64,512]{2,1,0:T(8,128)S(1)}, f32[10,64,512]{2,1,0:T(8,128)}, u32[]{:S(2)}, u32[]{:S(2)}) %collective-permute-start) | collective-permute-done | bytes 1310752 | tf_op jit(solution)/shard_map/ppermute | solution.py:248
  448.7 28.1 %collective-permute-done.25 = f32[5,64,512]{2,1,0:T(8,128)S(1)} collective-permute-done((f32[5,64,512]{2,1,0:T(8,128)S(1)}, f32[5,64,512]{2,1,0:T(8,128)S(1)}, u32[]{:S(2)}, u32[]{:S(2)}) %collective-permute-start.25) | collective-permute-done | bytes 655392 | tf_op jit(solution)/shard_map/ppermute | solution.py:262
  479.6 25.3 %collective-permute-done.22 = f32[5,64,512]{2,1,0:T(8,128)S(1)} collective-permute-done((f32[5,64,512]{2,1,0:T(8,128)S(1)}, f32[5,64,512]{2,1,0:T(8,128)S(1)}, u32[]{:S(2)}, u32[]{:S(2)}) %collective-permute-start.22) | collective-permute-done | bytes 655392 | tf_op jit(solution)/shard_map/ppermute | solution.py:262
  507.7 24.8 %collective-permute-done.19 = f32[5,64,512]{2,1,0:T(8,128)S(1)} collective-permute-done((f32[5,64,512]{2,1,0:T(8,128)S(1)}, f32[5,64,512]{2,1,0:T(8,128)S(1)}, u32[]{:S(2)}, u32[]{:S(2)}) %collective-permute-start.19) | collective-permute-done | bytes 655392 | tf_op jit(solution)/shard_map/ppermute | solution.py:262
  532.8 13.7 %collective-permute-done.16 = f32[5,64,512]{2,1,0:T(8,128)S(1)} collective-permute-done((f32[5,64,512]{2,1,0:T(8,128)S(1)}, f32[5,64,512]{2,1,0:T(8,128)S(1)}, u32[]{:S(2)}, u32[]{:S(2)}) %collective-permute-start.16) | collective-permute-done | bytes 655392 | tf_op jit(solution)/shard_map/ppermute | solution.py:262
  546.8 32.3 %place_and_update.1 = f32[2560,1280]{1,0:T(8,128)} custom-call(s32[171]{0:T(256)S(1)} %concatenate.9.refs_0_, f32[10,64,512]{2,1,0:T(8,128)S(1)} %broadcast_select_fusion.3.refs_1_, f32[10,64,512]{2,1,0:T(8,128)} %copy-done.7, f32[10,64,512]{2,1,0:T(8,128)} %copy-done.6, f32[10,64,512]{2,1,0:T(8,128)} %copy-done.5, ...), custom_call_target="tpu_custom_call" | custom-call | flops 10066329600 | bytes 26214400 | tf_op jit(solution)/shard_map/place_and_update/pallas_call | solution.py:206
  (236 shorter events, 119.9 us)
Async XLA Ops:
  9.0 43.6 %all-to-all-start = ((s32[16,4,1]{1,2,0:T(1,128)}), s32[16,4,1]{1,2,0:T(1,128)S(1)}, u32[]{:S(2)}, u32[]{:S(2)}) async-start(s32[16,4,1]{1,2,0:T(1,128)} %bitcast.1), calls=%async_computation | async-start | bytes 16384 | tf_op jit(solution)/shard_map/all_to_all | solution.py:300
  52.6 86.3 %all-to-all-start.2 = ((f32[64,64,256]{2,1,0:T(8,128)}), f32[64,64,256]{2,1,0:T(8,128)}, u32[]{:S(2)}, u32[]{:S(2)}) async-start(f32[64,64,256]{2,1,0:T(8,128)} %copy-done.4), calls=%async_computation.2 | async-start | bytes 8388608 | tf_op jit(solution)/shard_map/all_to_all | solution.py:303
  59.8 78.3 %all-reduce.3.cloned.1.call-start = ((), (), s32[]{:S(2)}) async-start(), calls=%async_computation.5 | async-start | bytes 262144 | tf_op jit(solution)/shard_map/psum | solution.py:334
  61.5 144.5 %all-gather.4.cloned.1.call-start = ((), (), s32[]{:S(2)}) async-start(), calls=%async_computation.6 | async-start | bytes 1179648 | tf_op jit(solution)/shard_map/all_gather | solution.py:334
  138.1 140.1 %all-gather.6.cloned.1.call-start = ((), (), s32[]{:S(2)}) async-start(), calls=%async_computation.7 | async-start | bytes 5898240 | tf_op jit(solution)/shard_map/all_gather | solution.py:336
  138.9 55.9 %all-to-all-start.3 = ((f32[64,64,256]{2,1,0:T(8,128)}), f32[64,64,256]{2,1,0:T(8,128)}, u32[]{:S(2)}, u32[]{:S(2)}) async-start(f32[64,64,256]{2,1,0:T(8,128)} %copy-done.3), calls=%async_computation.3 | async-start | bytes 8388608 | tf_op jit(solution)/shard_map/all_to_all | solution.py:303
  194.8 73.7 %all-to-all-start.4 = ((f32[64,64,256]{2,1,0:T(8,128)}), f32[64,64,256]{2,1,0:T(8,128)}, u32[]{:S(2)}, u32[]{:S(2)}) async-start(f32[64,64,256]{2,1,0:T(8,128)} %copy-done.2), calls=%async_computation.4 | async-start | bytes 8388608 | tf_op jit(solution)/shard_map/all_to_all | solution.py:303
  268.5 110.8 %all-to-all-start.1 = ((f32[64,64,256]{2,1,0:T(8,128)}), f32[64,64,256]{2,1,0:T(8,128)}, u32[]{:S(2)}, u32[]{:S(2)}) async-start(f32[64,64,256]{2,1,0:T(8,128)} %copy-done.1), calls=%async_computation.1 | async-start | bytes 8388608 | tf_op jit(solution)/shard_map/all_to_all | solution.py:303
  290.4 54.1 %collective-permute-start.14 = (f32[10,64,512]{2,1,0:T(8,128)}, f32[10,64,512]{2,1,0:T(8,128)}, u32[]{:S(2)}, u32[]{:S(2)}) collective-permute-start(f32[10,64,512]{2,1,0:T(8,128)} %slab_strip.7), channel_id=1, source_target_pairs={{0,4},{8,12},{16,20},{24,28},{32,36},{40,44},{48,52},{56,60},{64,6... | collective-permute-start | bytes 3932168 | tf_op jit(solution)/shard_map/ppermute | solution.py:248
  292.1 53.8 %collective-permute-start.13 = (f32[10,64,512]{2,1,0:T(8,128)}, f32[10,64,512]{2,1,0:T(8,128)}, u32[]{:S(2)}, u32[]{:S(2)}) collective-permute-start(f32[10,64,512]{2,1,0:T(8,128)} %slab_strip.7), channel_id=1, source_target_pairs={{0,6},{8,14},{16,22},{24,30},{32,38},{40,46},{48,54},{56,62},{64,7... | collective-permute-start | bytes 3932168 | tf_op jit(solution)/shard_map/ppermute | solution.py:248
  293.8 53.8 %collective-permute-start.12 = (f32[10,64,512]{2,1,0:T(8,128)}, f32[10,64,512]{2,1,0:T(8,128)}, u32[]{:S(2)}, u32[]{:S(2)}) collective-permute-start(f32[10,64,512]{2,1,0:T(8,128)} %slab_strip.7), channel_id=1, source_target_pairs={{0,2},{8,10},{16,18},{24,26},{32,34},{40,42},{48,50},{56,58},{64,6... | collective-permute-start | bytes 3932168 | tf_op jit(solution)/shard_map/ppermute | solution.py:248
  334.6 41.6 %collective-permute-start.10 = (f32[10,64,512]{2,1,0:T(8,128)}, f32[10,64,512]{2,1,0:T(8,128)}, u32[]{:S(2)}, u32[]{:S(2)}) collective-permute-start(f32[10,64,512]{2,1,0:T(8,128)} %slab_strip.6), channel_id=1, source_target_pairs={{0,4},{8,12},{16,20},{24,28},{32,36},{40,44},{48,52},{56,60},{64,6... | collective-permute-start | bytes 3932168 | tf_op jit(solution)/shard_map/ppermute | solution.py:248
  339.2 40.8 %collective-permute-start.9 = (f32[10,64,512]{2,1,0:T(8,128)}, f32[10,64,512]{2,1,0:T(8,128)}, u32[]{:S(2)}, u32[]{:S(2)}) collective-permute-start(f32[10,64,512]{2,1,0:T(8,128)} %slab_strip.6), channel_id=1, source_target_pairs={{0,6},{8,14},{16,22},{24,30},{32,38},{40,46},{48,54},{56,62},{64,7... | collective-permute-start | bytes 3932168 | tf_op jit(solution)/shard_map/ppermute | solution.py:248
  344.5 37.7 %collective-permute-start.8 = (f32[10,64,512]{2,1,0:T(8,128)}, f32[10,64,512]{2,1,0:T(8,128)}, u32[]{:S(2)}, u32[]{:S(2)}) collective-permute-start(f32[10,64,512]{2,1,0:T(8,128)} %slab_strip.6), channel_id=1, source_target_pairs={{0,2},{8,10},{16,18},{24,26},{32,34},{40,42},{48,50},{56,58},{64,6... | collective-permute-start | bytes 3932168 | tf_op jit(solution)/shard_map/ppermute | solution.py:248
  345.9 38.1 %collective-permute-start.6 = (f32[10,64,512]{2,1,0:T(8,128)}, f32[10,64,512]{2,1,0:T(8,128)}, u32[]{:S(2)}, u32[]{:S(2)}) collective-permute-start(f32[10,64,512]{2,1,0:T(8,128)} %slab_strip.5), channel_id=1, source_target_pairs={{0,4},{8,12},{16,20},{24,28},{32,36},{40,44},{48,52},{56,60},{64,6... | collective-permute-start | bytes 3932168 | tf_op jit(solution)/shard_map/ppermute | solution.py:248
  347.7 41.5 %collective-permute-start.5 = (f32[10,64,512]{2,1,0:T(8,128)}, f32[10,64,512]{2,1,0:T(8,128)}, u32[]{:S(2)}, u32[]{:S(2)}) collective-permute-start(f32[10,64,512]{2,1,0:T(8,128)} %slab_strip.5), channel_id=1, source_target_pairs={{0,6},{8,14},{16,22},{24,30},{32,38},{40,46},{48,54},{56,62},{64,7... | collective-permute-start | bytes 3932168 | tf_op jit(solution)/shard_map/ppermute | solution.py:248
  384.0 50.8 %collective-permute-start = (f32[10,64,512]{2,1,0:T(8,128)S(1)}, f32[10,64,512]{2,1,0:T(8,128)}, u32[]{:S(2)}, u32[]{:S(2)}) collective-permute-start(f32[10,64,512]{2,1,0:T(8,128)S(1)} %slab_strip.4), channel_id=1, source_target_pairs={{0,2},{8,10},{16,18},{24,26},{32,34},{40,42},{48,50},{56,58},{64,6... | collective-permute-start | bytes 3932168 | tf_op jit(solution)/shard_map/ppermute | solution.py:248
  389.1 49.8 %collective-permute-start.15 = (f32[10,64,512]{2,1,0:T(8,128)}, f32[10,64,512]{2,1,0:T(8,128)}, u32[]{:S(2)}, u32[]{:S(2)}) collective-permute-start(f32[10,64,512]{2,1,0:T(8,128)} %add_select_fusion), channel_id=1, source_target_pairs={{0,1},{2,3},{4,5},{6,7},{8,9},{10,11},{12,13},{14,15},{16,17},{18,... | collective-permute-start | bytes 3932168 | tf_op jit(solution)/shard_map/ppermute | solution.py:250
  406.7 35.4 %collective-permute-start.11 = (f32[10,64,512]{2,1,0:T(8,128)S(1)}, f32[10,64,512]{2,1,0:T(8,128)S(1)}, u32[]{:S(2)}, u32[]{:S(2)}) collective-permute-start(f32[10,64,512]{2,1,0:T(8,128)S(1)} %add_select_fusion.1), channel_id=1, source_target_pairs={{0,1},{2,3},{4,5},{6,7},{8,9},{10,11},{12,13},{14,15},{16,17},{18,... | collective-permute-start | bytes 3932168 | tf_op jit(solution)/shard_map/ppermute | solution.py:250
  445.8 59.1 %collective-permute-start.22 = (f32[5,64,512]{2,1,0:T(8,128)S(1)}, f32[5,64,512]{2,1,0:T(8,128)S(1)}, u32[]{:S(2)}, u32[]{:S(2)}) collective-permute-start(f32[5,64,512]{2,1,0:T(8,128)S(1)} %constant_dynamic-slice_fusion.3), channel_id=1, source_target_pairs={{0,24},{1,25},{10,2},{11,3},{20,12},{21,13},{30,22},{31,23},{32,56... | collective-permute-start | bytes 1966088 | tf_op jit(solution)/shard_map/ppermute | solution.py:262
  447.1 58.5 %collective-permute-start.21 = (f32[5,64,512]{2,1,0:T(8,128)S(1)}, f32[5,64,512]{2,1,0:T(8,128)S(1)}, u32[]{:S(2)}, u32[]{:S(2)}) collective-permute-start(f32[5,64,512]{2,1,0:T(8,128)S(1)} %constant_dynamic-slice_fusion.4), channel_id=1, source_target_pairs={{0,8},{1,9},{10,18},{11,19},{20,28},{21,29},{30,6},{31,7},{32,40},... | collective-permute-start | bytes 1966088 | tf_op jit(solution)/shard_map/ppermute | solution.py:262
  477.5 55.0 %collective-permute-start.19 = (f32[5,64,512]{2,1,0:T(8,128)S(1)}, f32[5,64,512]{2,1,0:T(8,128)S(1)}, u32[]{:S(2)}, u32[]{:S(2)}) collective-permute-start(f32[5,64,512]{2,1,0:T(8,128)S(1)} %constant_dynamic-slice_fusion.4), channel_id=1, source_target_pairs={{0,24},{1,25},{10,2},{11,3},{20,12},{21,13},{30,22},{31,23},{32,56... | collective-permute-start | bytes 1966088 | tf_op jit(solution)/shard_map/ppermute | solution.py:262
  478.9 53.9 %collective-permute-start.18 = (f32[5,64,512]{2,1,0:T(8,128)S(1)}, f32[5,64,512]{2,1,0:T(8,128)S(1)}, u32[]{:S(2)}, u32[]{:S(2)}) collective-permute-start(f32[5,64,512]{2,1,0:T(8,128)S(1)} %constant_dynamic-slice_fusion.5), channel_id=1, source_target_pairs={{0,8},{1,9},{10,18},{11,19},{20,28},{21,29},{30,6},{31,7},{32,40},... | collective-permute-start | bytes 1966088 | tf_op jit(solution)/shard_map/ppermute | solution.py:262
  505.6 41.0 %collective-permute-start.16 = (f32[5,64,512]{2,1,0:T(8,128)S(1)}, f32[5,64,512]{2,1,0:T(8,128)S(1)}, u32[]{:S(2)}, u32[]{:S(2)}) collective-permute-start(f32[5,64,512]{2,1,0:T(8,128)S(1)} %constant_dynamic-slice_fusion.5), channel_id=1, source_target_pairs={{0,24},{1,25},{10,2},{11,3},{20,12},{21,13},{30,22},{31,23},{32,56... | collective-permute-start | bytes 1966088 | tf_op jit(solution)/shard_map/ppermute | solution.py:262
  (38 other events, 796.8 us)
Sparse Core Ops, SparseCore 0:
  63.0 75.0 all-reduce.2
  139.9 21.9 all-gather.3
  163.7 37.1 all-gather.5

commit v2 on v1

--- a/solution.py
+++ b/solution.py
@@ -9,7 +9,7 @@
 BS = 256
 CAP = 4
 PIV = 512
-STRIPS = (64, 64, 64, 64)
+STRIPS = (64, 64, 64, 32, 32)
 OFFSETS = tuple(sum(STRIPS[:q]) for q in range(len(STRIPS)))
 NSTRIP = len(STRIPS)
 RING = 8
@@ -22,30 +22,36 @@
     return jnp.tril(block) + jnp.tril(block, -1).T
 
 
-def permute_kernel(slot_ref, tile_ref, rows_ref, cols_ref, *out_refs):
+def permute_kernel(first, heights, slot_ref, tile_ref, rows_ref, cols_ref, *out_refs):
     tile = tile_ref[0]
     high = tile.astype(bf16)
     rest = tile - high.astype(f32)
     mid = rest.astype(bf16)
     low = (rest - mid.astype(f32)).astype(bf16)
+    parts = jnp.concatenate([high, mid, low], axis=1)
+    count = sum(heights)
+    half = BS // 2
+    wanted = jnp.transpose(jnp.broadcast_to(rows_ref[0], (half, BS)))[first : first + count]
+    lane = lax.broadcasted_iota(i32, (count, half), 1)
+    pick_rows = jnp.concatenate(
+        [jnp.where(wanted == lane + k * half, 1.0, 0.0) for k in range(2)], axis=1
+    ).astype(bf16)
     place = lax.broadcasted_iota(i32, (BS, BS), 0)
-    pick_rows = jnp.where(place == rows_ref[0], 1.0, 0.0).astype(bf16)
     pick_cols = jnp.where(place == cols_ref[0], 1.0, 0.0).astype(bf16)
-    parts = jnp.concatenate([high, mid, low], axis=1)
-    moved = lax.dot_general(
-        pick_rows, parts, (((0,), (0,)), ((), ())), preferred_element_type=f32
-    ).astype(bf16)
+    moved = jnp.dot(pick_rows, parts, preferred_element_type=f32).astype(bf16)
     out = jnp.dot(moved[:, :BS], pick_cols, preferred_element_type=f32)
     out = out + jnp.dot(moved[:, BS : 2 * BS], pick_cols, preferred_element_type=f32)
     out = out + jnp.dot(moved[:, 2 * BS :], pick_cols, preferred_element_type=f32)
-    for q, out_ref in enumerate(out_refs):
-        out_ref[0] = out[OFFSETS[q] : OFFSETS[q] + STRIPS[q]]
-
-
-def permute(slot, tiles, rows_from, cols_from, slots):
+    at = 0
+    for out_ref, h in zip(out_refs, heights, strict=True):
+        out_ref[0] = out[at : at + h]
+        at += h
+
+
+def permute(slot, tiles, rows_from, cols_from, slots, first, heights):
     count = tiles.shape[0]
     return pl.pallas_call(
-        permute_kernel,
+        lambda *refs: permute_kernel(first, heights, *refs),
         grid_spec=pltpu.PrefetchScalarGridSpec(
             num_scalar_prefetch=1,
             grid=(count,),
@@ -55,31 +61,35 @@
                 pl.BlockSpec((1, 1, BS), lambda t, slot: (t, 0, 0)),
             ],
             out_specs=[
-                pl.BlockSpec((1, h, BS), lambda t, slot: (slot[t], 0, 0)) for h in STRIPS
+                pl.BlockSpec((1, h, BS), lambda t, slot: (slot[t], 0, 0)) for h in heights
             ],
         ),
-        out_shape=[jax.ShapeDtypeStruct((slots, h, BS), f32) for h in STRIPS],
-        compiler_params=pltpu.CompilerParams(vmem_limit_bytes=32 << 20),
+        out_shape=[jax.ShapeDtypeStruct((slots, h, BS), f32) for h in heights],
+        compiler_params=pltpu.CompilerParams(vmem_limit_bytes=58 << 20),
         cost_estimate=pl.CostEstimate(
-            flops=12 * count * BS**3, bytes_accessed=8 * count * BS * BS, transcendentals=0
+            flops=12 * count * BS * BS * sum(heights),
+            bytes_accessed=4 * count * BS * (BS + sum(heights)),
+            transcendentals=0,
         ),
         name="permute_tiles",
     )(slot, tiles, rows_from[:, None, :], cols_from[:, None, :])
 
 
-def slab_kernel(height, meta, initial_ref, in_ref, out_ref, ring, sems):
+def slab_kernel(first, height, meta, initial_ref, in_ref, out_ref, ring, sems, initial_sem):
     total = meta[128]
 
     def copy(g):
         return pltpu.make_async_copy(in_ref.at[meta[g]], ring.at[g % RING], sems.at[g % RING])
 
+    begin = pltpu.make_async_copy(initial_ref.at[:, pl.ds(first, height)], out_ref, initial_sem)
+    begin.start()
     for g in range(RING):
 
         @pl.when(g < total)
         def _():
             copy(g).start()
 
-    out_ref[...] = initial_ref[...]
+    begin.wait()
 
     @pl.loop(0, total)
     def _(g):
@@ -93,21 +103,19 @@
             copy(g + RING).start()
 
 
-def slab_strip(meta, initial, incoming, height):
+def slab_strip(meta, initial, incoming, first, height):
     blocks = initial.shape[0]
     return pl.pallas_call(
-        lambda *refs: slab_kernel(height, *refs),
+        lambda *refs: slab_kernel(first, height, *refs),
         grid_spec=pltpu.PrefetchScalarGridSpec(
             num_scalar_prefetch=1,
             grid=(1,),
-            in_specs=[
-                pl.BlockSpec((blocks, height, PIV), lambda i, meta: (0, 0, 0)),
-                pl.BlockSpec(memory_space=pl.ANY),
-            ],
+            in_specs=[pl.BlockSpec(memory_space=pl.ANY)] * 2,
             out_specs=pl.BlockSpec((blocks, height, PIV), lambda i, meta: (0, 0, 0)),
             scratch_shapes=[
                 pltpu.VMEM((RING, height, BS), f32),
                 pltpu.SemaphoreType.DMA((RING,)),
+                pltpu.SemaphoreType.DMA(()),
             ],
         ),
         out_shape=jax.ShapeDtypeStruct((blocks, height, PIV), f32),
@@ -231,17 +239,33 @@
     )(meta, *slab, *across, *mats, *incoming)
 
 
-def factors(corner, keep):
-    first = jnp.linalg.cholesky(lower_sym(corner[:BS, :BS]))
-    eye = jnp.eye(BS, dtype=f32)
-    first_inv = lax.linalg.triangular_solve(first, eye, left_side=True, lower=True)
-    below = jnp.dot(corner[BS:, :BS], first_inv.T, precision=HIGH)
-    below = jnp.where(keep, below, jnp.zeros_like(below))
-    rest = corner[BS:, BS:] - jnp.dot(below, below.T, precision=HIGH)
-    second = jnp.linalg.cholesky(lower_sym(rest))
-    second_inv = lax.linalg.triangular_solve(second, eye, left_side=True, lower=True)
-    cross = jnp.dot(below.T, second_inv.T, precision=HIGH)
-    return first_inv.T, second_inv.T, cross, first, second
+def dot(a, b):
+    return jnp.dot(a, b, precision=HIGH)
+
+
+def inverse(lower):
+    size = lower.shape[0]
+    eye = jnp.eye(size, dtype=f32)
+    scale = jnp.sum(lower * eye, axis=0)
+    power = eye - lower / scale[None, :]
+    out = eye + power
+    for _ in range(6):
+        power = dot(power, power)
+        out = out + dot(power, out)
+    return out / scale[:, None]
+
+
+def panel(block):
+    half = BS // 2
+    first = jnp.linalg.cholesky(lower_sym(block[:half, :half]))
+    first_inv = inverse(first)
+    below = dot(block[half:, :half], first_inv.T)
+    second = jnp.linalg.cholesky(lower_sym(block[half:, half:] - dot(below, below.T)))
+    second_inv = inverse(second)
+    across = -dot(second_inv, dot(below, first_inv))
+    zero = jnp.zeros((half, half), f32)
+    factor = jnp.block([[first, zero], [below, second]])
+    return factor, jnp.block([[first_inv.T, across.T], [zero, second_inv.T]])
 
 
 def spread_col(x, my_col):
@@ -254,14 +278,19 @@
 def spread_row(x, my_row, my_col, n_row, n_col):
     half = x.shape[0] // 2
     own = lax.dynamic_slice_in_dim(x, (my_col % 2) * half, half, 0)
-    out = own
-    for step in range(1, n_row):
-        pairs = [
-            ((c // 2) * n_col + c, ((c // 2 + step) % n_row) * n_col + c) for c in range(n_col)
+
+    def pairs(start, stop):
+        return [
+            ((c // 2 + start[c % 2]) % n_row * n_col + c, (c // 2 + stop) % n_row * n_col + c)
+            for c in range(n_col)
         ]
-        got = lax.ppermute(own, ("row", "col"), pairs)
-        out = jnp.where((my_row - my_col // 2) % n_row == step, got, out)
-    return out
+
+    step = (my_row - my_col // 2) % n_row
+    after = lax.ppermute(own, ("row", "col"), pairs((0, 0), 1))
+    before = lax.ppermute(own, ("row", "col"), pairs((0, 0), -1))
+    near = jnp.where(step == 0, own, jnp.where(step == 1, after, before))
+    far = lax.ppermute(near, ("row", "col"), pairs((1, -1), 2))
+    return jnp.where(step == 2, far, near)
 
 
 def ordered(key, valid, span):
@@ -298,11 +327,6 @@
         jnp.any(choose, axis=1), jnp.sum(jnp.where(choose, block_id[None, :], 0), axis=1), -1
     )
     names = lax.all_to_all(labels, ("front", "row"), split_axis=0, concat_axis=0, tiled=True)
-    outgoing = permute(slot, tiles, rows_from, cols_from, slots)
-    incoming = [
-        lax.all_to_all(part, ("front", "row"), split_axis=0, concat_axis=0, tiled=True)
-        for part in outgoing
-    ]
     valid = names >= 0
     order, sorted_id, key = ordered(names, valid, row_blocks * col_blocks)
     bounds = jnp.arange(row_blocks + 1, dtype=i32)[:, None] * col_blocks
@@ -330,19 +354,43 @@
         ]
     )
 
-    pivot = jnp.where(my_row == 0, initial[0, :PIV], 0.0)
-    corner = lax.all_gather(lax.psum(pivot, "row"), "col", axis=1, tiled=True)
-    mats = factors(corner, pattern[0, 0, 1] == 1)
+    corner = lax.all_gather(initial[0, :PIV], ("row", "col"), axis=0)[:n_col]
+    corner = corner.transpose(1, 0, 2).reshape(PIV, PIV)
     columns = lax.all_gather(initial[0], "col", axis=1, tiled=True)
     columns = columns.reshape(row_blocks, BS, PIV)
 
-    slab, across = [], []
-    for q in range(NSTRIP):
-        rows = slice(OFFSETS[q], OFFSETS[q] + STRIPS[q])
-        strip = slab_strip(slab_meta, columns[:, rows], incoming[q], STRIPS[q])
-        strip = spread_col(strip, my_col)
-        slab.append(strip)
-        across.append(spread_row(strip, my_row, my_col, n_row, n_col))
+    def send(part):
+        return lax.all_to_all(part, ("front", "row"), split_axis=0, concat_axis=0, tiled=True)
+
+    outgoing = permute(slot, tiles, rows_from, cols_from, slots, 0, STRIPS[:1])
+    outgoing += permute(slot, tiles, rows_from, cols_from, slots, STRIPS[0], STRIPS[1:])
+    incoming, slab, across = [], [], []
+
+    def collect(q):
+        strip = slab_strip(slab_meta, columns, incoming[q], OFFSETS[q], STRIPS[q])
+        slab.append(spread_col(strip, my_col))
+        across.append(spread_row(slab[q], my_row, my_col, n_row, n_col))
+
+    incoming.append(send(outgoing[0]))
+    incoming.append(send(outgoing[1]))
+    collect(0)
+    first, first_inv = panel(corner[:BS, :BS])
+    below = dot(corner[BS:, :BS], first_inv)
+    below = jnp.where(pattern[0, 0, 1] == 1, below, jnp.zeros_like(below))
+    rest = corner[BS:, BS:] - dot(below, below.T)
+    part, slab[0], rest = lax.optimization_barrier((outgoing[2], slab[0], rest))
+    incoming.append(send(part))
+    collect(1)
+    second, second_inv = panel(rest)
+    cross = dot(below.T, second_inv)
+    mats = (first_inv, second_inv, cross, first, second)
+    part, slab[1], across[0], mats = lax.optimization_barrier((outgoing[3], slab[1], across[0], mats))
+    incoming.append(send(part))
+    collect(2)
+    part, across[1] = lax.optimization_barrier((outgoing[4], across[1]))
+    incoming.append(send(part))
+    collect(3)
+    collect(4)
     return final(meta, slab, across, mats, incoming, row_blocks, col_blocks)[None]
 
 

time: 594 us -> 545 us (0.918)
  the two profiles are of different devices: /device:TPU:10 before, /device:TPU:64 now
where the time goes in v2:
time: 545 us; the launch traced here: 535 us
  waiting for transfers between devices  179 us (33%)
  starting transfers between devices  105 us (19%)
  Pallas kernels  96.6 us (18%)
  other arithmetic  85.7 us (16%)
  local copies, waits for them, and re-layouts  34.1 us (6%)
  matrix products  18.3 us (3%)
  between operations  16 us (3%)
    ppermute x5, waiting for transfers between devices, spread_row(): far = lax.ppermute(near, ('row', 'col'), pairs((1, -1), 2))  92.2 us
    pallas_call x2, Pallas kernels, permute(): pl.pallas_call(lambda *refs: permute_kernel(first, heights, *refs), grid_...  51.5 us
    all_to_all x5, waiting for transfers between devices, send(): lax.all_to_all(part, ('front', 'row'), split_axis=0, concat_axis=0, tiled...  49.7 us
    all_to_all x5, starting transfers between devices, send(): lax.all_to_all(part, ('front', 'row'), split_axis=0, concat_axis=0, tiled...  39.3 us
    ppermute x15, waiting for transfers between devices, spread_col(): arrived = [lax.ppermute(x, 'col', [(0, to)]) for to in (2, 6, 4)]  36.5 us
    ppermute x15, starting transfers between devices, spread_col(): arrived = [lax.ppermute(x, 'col', [(0, to)]) for to in (2, 6, 4)]  32.9 us
    pallas_call x1, Pallas kernels, final(): pl.pallas_call(lambda *refs: final_kernel(col_blocks, *refs), grid_spec=p...  32.9 us
    another operation x6, other arithmetic, panel(): jnp.linalg.cholesky(lower_sym(block[half:, half:] - dot(below, below.T)))  27.1 us
  transfers between devices with their start and end apart: 43, of which 16 were waited for; matrix products, arithmetic and copies ran while one was open for 23% of the time, Pallas kernels for 12%

profile of v2, /device:TPU:64, one launch (start us, length us, event | category | flops | bytes accessed | tf_op | source)
XLA Modules:
  0.0 534.8 jit_solution(10726602773403816068)
XLA Ops:
  11.4 7.4 %all-to-all-start = ((s32[16,4,1]{1,2,0:T(1,128)}), s32[16,4,1]{1,2,0:T(1,128)S(1)}, u32[]{:S(2)}, u32[]{:S(2)}) async-start(s32[16,4,1]{1,2,0:T(1,128)} %bitcast.1), calls=%async_computation | async-start | bytes 16384 | tf_op jit(solution)/shard_map/all_to_all | solution.py:329
  22.9 24.8 %permute_tiles.3 = f32[64,64,256]{2,1,0:T(8,128)} custom-call(s32[32]{0:T(128)} %copy-done.27, f32[32,256,256]{2,1,0:T(8,128)} %refs_1_.3, s32[32,1,256]{2,1,0:T(1,128)} %broadcast_in_dim.147.refs_2_, s32[32,1,256]{2,1,0:T(1,128)} %broadcast_in_dim.148.refs_3_), custom_call_target="tpu_custom_call" | custom-call | flops 1610612736 | bytes 10485760 | tf_op jit(solution)/shard_map/permute_tiles/pallas_call | solution.py:53
  47.7 26.7 %permute_tiles.2 = (f32[64,64,256]{2,1,0:T(8,128)}, f32[64,64,256]{2,1,0:T(8,128)}, f32[64,32,256]{2,1,0:T(8,128)}, f32[64,32,256]{2,1,0:T(8,128)}) custom-call(s32[32]{0:T(128)} %copy-done.27, f32[32,256,256]{2,1,0:T(8,128)} %refs_1_.3, s32[32,1,256]{2,1,0:T(1,128)} %broadcast_in_dim.147.refs_2_, s32[32,1,256]{2,1,0:T(1,128)} %broadcast_in_dim.148.refs_3_), custom_call_target="tpu_custom_call" | custom-call | flops 4831838208 | bytes 14680064 | tf_op jit(solution)/shard_map/permute_tiles/pallas_call | solution.py:53
  75.7 7.3 %all-to-all-start.1 = ((f32[64,64,256]{2,1,0:T(8,128)}), f32[64,64,256]{2,1,0:T(8,128)}, u32[]{:S(2)}, u32[]{:S(2)}) async-start(f32[64,64,256]{2,1,0:T(8,128)} %permute_tiles.3), calls=%async_computation.1 | async-start | bytes 8388608 | tf_op jit(solution)/shard_map/all_to_all | solution.py:363
  88.6 11.7 %cholesky.74 = f32[128,128]{1,0:T(8,128)S(1)} custom-call(f32[128,128]{1,0:T(8,128)S(1)} %copy.166), custom_call_target="Cholesky" | custom-call | tf_op jit(solution)/shard_map/jit(cholesky)/cholesky | solution.py:260
  104.5 33.3 %all-to-all-done.1.refs_2_.refs_16_ = f32[64,64,256]{2,1,0:T(8,128)} async-done(((f32[64,64,256]{2,1,0:T(8,128)}), f32[64,64,256]{2,1,0:T(8,128)}, u32[]{:S(2)}, u32[]{:S(2)}) %all-to-all-start.1) | async-done | bytes 4194336 | tf_op jit(solution)/shard_map/all_to_all | solution.py:363
  137.8 11.9 %all-to-all-start.2 = ((f32[64,64,256]{2,1,0:T(8,128)}), f32[64,64,256]{2,1,0:T(8,128)}, u32[]{:S(2)}, u32[]{:S(2)}) async-start(f32[64,64,256]{2,1,0:T(8,128)} %get-tuple-element.26), calls=%async_computation.2 | async-start | bytes 8388608 | tf_op jit(solution)/shard_map/all_to_all | solution.py:363
  150.5 11.7 %cholesky.85 = f32[128,128]{1,0:T(8,128)S(1)} custom-call(f32[128,128]{1,0:T(8,128)S(1)} %copy.171), custom_call_target="Cholesky" | custom-call | tf_op jit(solution)/shard_map/jit(cholesky)/cholesky | solution.py:263
  165.2 5.9 %copy.162 = f32[1,2560,512]{2,1,0:T(8,128)} copy(f32[1,2560,512]{1,2,0:T(8,128)} %all-gather.6.cloned.1.call-done) | data formatting | bytes 10485760 | tf_op jit(solution)/shard_map/all_gather | solution.py:359
  184.5 15.8 %all-to-all-done.2.refs_2_.refs_17_ = f32[64,64,256]{2,1,0:T(8,128)} async-done(((f32[64,64,256]{2,1,0:T(8,128)}), f32[64,64,256]{2,1,0:T(8,128)}, u32[]{:S(2)}, u32[]{:S(2)}) %all-to-all-start.2) | async-done | bytes 4194336 | tf_op jit(solution)/shard_map/all_to_all | solution.py:363
  216.4 5.4 %collective-permute-done.6 = f32[10,64,512]{2,1,0:T(8,128)S(1)} collective-permute-done((f32[10,64,512]{2,1,0:T(8,128)S(1)}, f32[10,64,512]{2,1,0:T(8,128)S(1)}, u32[]{:S(2)}, u32[]{:S(2)}) %collective-permute-start.6) | collective-permute-done | bytes 1310752 | tf_op jit(solution)/shard_map/ppermute | solution.py:272
  223.2 12.7 %collective-permute-done.4 = f32[10,64,512]{2,1,0:T(8,128)S(1)} collective-permute-done((f32[10,64,512]{2,1,0:T(8,128)S(1)}, f32[10,64,512]{2,1,0:T(8,128)S(1)}, u32[]{:S(2)}, u32[]{:S(2)}) %collective-permute-start.4) | collective-permute-done | bytes 1310752 | tf_op jit(solution)/shard_map/ppermute | solution.py:272
  243.8 11.7 %cholesky.96 = f32[128,128]{1,0:T(8,128)S(1)} custom-call(f32[128,128]{1,0:T(8,128)S(1)} %copy.182), custom_call_target="Cholesky" | custom-call | tf_op jit(solution)/shard_map/jit(cholesky)/cholesky | solution.py:260
  263.1 33.6 %collective-permute-done.21 = f32[5,64,512]{2,1,0:T(8,128)S(1)} collective-permute-done((f32[5,64,512]{2,1,0:T(8,128)S(1)}, f32[5,64,512]{2,1,0:T(8,128)S(1)}, u32[]{:S(2)}, u32[]{:S(2)}) %collective-permute-start.21) | collective-permute-done | bytes 655392 | tf_op jit(solution)/shard_map/ppermute | solution.py:292
  297.6 6.3 %all-to-all-start.5 = ((f32[64,32,256]{2,1,0:T(8,128)}), f32[64,32,256]{2,1,0:T(8,128)S(1)}, u32[]{:S(2)}, u32[]{:S(2)}) async-start(f32[64,32,256]{2,1,0:T(8,128)} %get-tuple-element.32), calls=%async_computation.5 | async-start | bytes 4194304 | tf_op jit(solution)/shard_map/all_to_all | solution.py:363
  314.8 13.2 %cholesky.107 = f32[128,128]{1,0:T(8,128)} custom-call(f32[128,128]{1,0:T(8,128)} %fusion.7), custom_call_target="Cholesky" | custom-call | tf_op jit(solution)/shard_map/jit(cholesky)/cholesky | solution.py:263
  332.6 7.8 %all-to-all-start.3 = ((f32[64,64,256]{2,1,0:T(8,128)}), f32[64,64,256]{2,1,0:T(8,128)}, u32[]{:S(2)}, u32[]{:S(2)}) async-start(f32[64,64,256]{2,1,0:T(8,128)} %get-tuple-element.29), calls=%async_computation.3 | async-start | bytes 8388608 | tf_op jit(solution)/shard_map/all_to_all | solution.py:363
  348.6 28.4 %collective-permute-done.10 = f32[5,64,512]{2,1,0:T(8,128)S(1)} collective-permute-done((f32[5,64,512]{2,1,0:T(8,128)S(1)}, f32[5,64,512]{2,1,0:T(8,128)S(1)}, u32[]{:S(2)}, u32[]{:S(2)}) %collective-permute-start.10) | collective-permute-done | bytes 655392 | tf_op jit(solution)/shard_map/ppermute | solution.py:292
  378.0 6.1 %all-to-all-start.4 = ((f32[64,32,256]{2,1,0:T(8,128)}), f32[64,32,256]{2,1,0:T(8,128)}, u32[]{:S(2)}, u32[]{:S(2)}) async-start(f32[64,32,256]{2,1,0:T(8,128)} %get-tuple-element.30), calls=%async_computation.4 | async-start | bytes 4194304 | tf_op jit(solution)/shard_map/all_to_all | solution.py:363
  413.2 4.2 collective-permute-start.17
  440.6 7.0 %collective-permute-done.15 = f32[10,32,512]{2,1,0:T(8,128)S(1)} collective-permute-done((f32[10,32,512]{2,1,0:T(8,128)S(1)}, f32[10,32,512]{2,1,0:T(8,128)S(1)}, u32[]{:S(2)}, u32[]{:S(2)}) %collective-permute-start.15) | collective-permute-done | bytes 655392 | tf_op jit(solution)/shard_map/ppermute | solution.py:272
  460.9 20.7 %collective-permute-done.34 = f32[5,32,512]{2,1,0:T(8,128)} collective-permute-done((f32[5,32,512]{2,1,0:T(8,128)S(1)}, f32[5,32,512]{2,1,0:T(8,128)}, u32[]{:S(2)}, u32[]{:S(2)}) %collective-permute-start.34) | collective-permute-done | bytes 327712 | tf_op jit(solution)/shard_map/ppermute | solution.py:292
  482.7 9.4 %collective-permute-done.31 = f32[5,32,512]{2,1,0:T(8,128)} collective-permute-done((f32[5,32,512]{2,1,0:T(8,128)S(1)}, f32[5,32,512]{2,1,0:T(8,128)}, u32[]{:S(2)}, u32[]{:S(2)}) %collective-permute-start.31) | collective-permute-done | bytes 327712 | tf_op jit(solution)/shard_map/ppermute | solution.py:292
  494.5 32.9 %place_and_update.1 = f32[2560,1280]{1,0:T(8,128)} custom-call(s32[171]{0:T(256)S(1)} %concatenate.45.refs_0_, f32[10,64,512]{2,1,0:T(8,128)} %copy-done.11, f32[10,64,512]{2,1,0:T(8,128)} %copy-done.12, f32[10,64,512]{2,1,0:T(8,128)} %copy-done.13, f32[10,32,512]{2,1,0:T(8,128)S(1)} %broadcast_select_fusion.4.refs_4_, ...), custom_call_target="tpu_custom_call" | custom-call | flops 10066329600 | bytes 26214400 | tf_op jit(solution)/shard_map/place_and_update/pallas_call | solution.py:214
  (303 shorter events, 162.7 us)
Async XLA Ops:
  6.5 80.4 %all-gather.4.cloned.1.call-start = ((), (), s32[]{:S(2)}) async-start(), calls=%async_computation.6 | async-start | bytes 4325376 | tf_op jit(solution)/shard_map/all_gather | solution.py:357
  8.1 157.0 %all-gather.6.cloned.1.call-start = ((), (), s32[]{:S(2)}) async-start(), calls=%async_computation.7 | async-start | bytes 5898240 | tf_op jit(solution)/shard_map/all_gather | solution.py:359
  11.4 64.3 %all-to-all-start = ((s32[16,4,1]{1,2,0:T(1,128)}), s32[16,4,1]{1,2,0:T(1,128)S(1)}, u32[]{:S(2)}, u32[]{:S(2)}) async-start(s32[16,4,1]{1,2,0:T(1,128)} %bitcast.1), calls=%async_computation | async-start | bytes 16384 | tf_op jit(solution)/shard_map/all_to_all | solution.py:329
  75.7 62.1 %all-to-all-start.1 = ((f32[64,64,256]{2,1,0:T(8,128)}), f32[64,64,256]{2,1,0:T(8,128)}, u32[]{:S(2)}, u32[]{:S(2)}) async-start(f32[64,64,256]{2,1,0:T(8,128)} %permute_tiles.3), calls=%async_computation.1 | async-start | bytes 8388608 | tf_op jit(solution)/shard_map/all_to_all | solution.py:363
  137.8 62.6 %all-to-all-start.2 = ((f32[64,64,256]{2,1,0:T(8,128)}), f32[64,64,256]{2,1,0:T(8,128)}, u32[]{:S(2)}, u32[]{:S(2)}) async-start(f32[64,64,256]{2,1,0:T(8,128)} %get-tuple-element.26), calls=%async_computation.2 | async-start | bytes 8388608 | tf_op jit(solution)/shard_map/all_to_all | solution.py:363
  176.1 32.1 %collective-permute-start.2 = (f32[10,64,512]{2,1,0:T(8,128)S(1)}, f32[10,64,512]{2,1,0:T(8,128)}, u32[]{:S(2)}, u32[]{:S(2)}) collective-permute-start(f32[10,64,512]{2,1,0:T(8,128)S(1)} %slab_strip.5), channel_id=1, source_target_pairs={{0,4},{8,12},{16,20},{24,28},{32,36},{40,44},{48,52},{56,60},{64,6... | collective-permute-start | bytes 3932168 | tf_op jit(solution)/shard_map/ppermute | solution.py:272
  178.5 31.0 %collective-permute-start.1 = (f32[10,64,512]{2,1,0:T(8,128)S(1)}, f32[10,64,512]{2,1,0:T(8,128)}, u32[]{:S(2)}, u32[]{:S(2)}) collective-permute-start(f32[10,64,512]{2,1,0:T(8,128)S(1)} %slab_strip.5), channel_id=1, source_target_pairs={{0,6},{8,14},{16,22},{24,30},{32,38},{40,46},{48,54},{56,62},{64,7... | collective-permute-start | bytes 3932168 | tf_op jit(solution)/shard_map/ppermute | solution.py:272
  180.9 28.7 %collective-permute-start = (f32[10,64,512]{2,1,0:T(8,128)S(1)}, f32[10,64,512]{2,1,0:T(8,128)}, u32[]{:S(2)}, u32[]{:S(2)}) collective-permute-start(f32[10,64,512]{2,1,0:T(8,128)S(1)} %slab_strip.5), channel_id=1, source_target_pairs={{0,2},{8,10},{16,18},{24,26},{32,34},{40,42},{48,50},{56,58},{64,6... | collective-permute-start | bytes 3932168 | tf_op jit(solution)/shard_map/ppermute | solution.py:272
  208.2 27.7 %collective-permute-start.4 = (f32[10,64,512]{2,1,0:T(8,128)S(1)}, f32[10,64,512]{2,1,0:T(8,128)S(1)}, u32[]{:S(2)}, u32[]{:S(2)}) collective-permute-start(f32[10,64,512]{2,1,0:T(8,128)S(1)} %slab_strip.6), channel_id=1, source_target_pairs={{0,2},{8,10},{16,18},{24,26},{32,34},{40,42},{48,50},{56,58},{64,6... | collective-permute-start | bytes 3932168 | tf_op jit(solution)/shard_map/ppermute | solution.py:272
  212.3 26.6 %collective-permute-start.3 = (f32[10,64,512]{2,1,0:T(8,128)S(1)}, f32[10,64,512]{2,1,0:T(8,128)S(1)}, u32[]{:S(2)}, u32[]{:S(2)}) collective-permute-start(f32[10,64,512]{2,1,0:T(8,128)S(1)} %add_select_fusion.2), channel_id=1, source_target_pairs={{0,1},{2,3},{4,5},{6,7},{8,9},{10,11},{12,13},{14,15},{16,17},{18,... | collective-permute-start | bytes 3932168 | tf_op jit(solution)/shard_map/ppermute | solution.py:274
  240.2 102.7 %collective-permute-start.9 = (f32[5,64,512]{2,1,0:T(8,128)}, f32[5,64,512]{2,1,0:T(8,128)}, u32[]{:S(2)}, u32[]{:S(2)}) collective-permute-start(f32[5,64,512]{2,1,0:T(8,128)} %constant_dynamic-slice_fusion.4), channel_id=1, source_target_pairs={{0,24},{1,25},{10,2},{11,3},{20,12},{21,13},{30,22},{31,23},{32,56... | collective-permute-start | bytes 1966088 | tf_op jit(solution)/shard_map/ppermute | solution.py:290
  241.7 101.2 %collective-permute-start.8 = (f32[5,64,512]{2,1,0:T(8,128)}, f32[5,64,512]{2,1,0:T(8,128)}, u32[]{:S(2)}, u32[]{:S(2)}) collective-permute-start(f32[5,64,512]{2,1,0:T(8,128)} %constant_dynamic-slice_fusion.4), channel_id=1, source_target_pairs={{0,8},{1,9},{10,18},{11,19},{20,28},{21,29},{30,6},{31,7},{32,40},... | collective-permute-start | bytes 1966088 | tf_op jit(solution)/shard_map/ppermute | solution.py:289
  260.5 36.2 %collective-permute-start.21 = (f32[5,64,512]{2,1,0:T(8,128)S(1)}, f32[5,64,512]{2,1,0:T(8,128)S(1)}, u32[]{:S(2)}, u32[]{:S(2)}) collective-permute-start(f32[5,64,512]{2,1,0:T(8,128)S(1)} %select_select_fusion.1), channel_id=1, source_target_pairs={{8,16},{25,17},{18,26},{3,27},{28,4},{13,5},{6,14},{23,15},{40,48}... | collective-permute-start | bytes 1966088 | tf_op jit(solution)/shard_map/ppermute | solution.py:292
  297.6 34.9 %all-to-all-start.5 = ((f32[64,32,256]{2,1,0:T(8,128)}), f32[64,32,256]{2,1,0:T(8,128)S(1)}, u32[]{:S(2)}, u32[]{:S(2)}) async-start(f32[64,32,256]{2,1,0:T(8,128)} %get-tuple-element.32), calls=%async_computation.5 | async-start | bytes 4194304 | tf_op jit(solution)/shard_map/all_to_all | solution.py:363
  332.6 45.4 %all-to-all-start.3 = ((f32[64,64,256]{2,1,0:T(8,128)}), f32[64,64,256]{2,1,0:T(8,128)}, u32[]{:S(2)}, u32[]{:S(2)}) async-start(f32[64,64,256]{2,1,0:T(8,128)} %get-tuple-element.29), calls=%async_computation.3 | async-start | bytes 8388608 | tf_op jit(solution)/shard_map/all_to_all | solution.py:363
  344.4 32.5 %collective-permute-start.10 = (f32[5,64,512]{2,1,0:T(8,128)S(1)}, f32[5,64,512]{2,1,0:T(8,128)S(1)}, u32[]{:S(2)}, u32[]{:S(2)}) collective-permute-start(f32[5,64,512]{2,1,0:T(8,128)S(1)} %select_select_fusion.2), channel_id=1, source_target_pairs={{8,16},{25,17},{18,26},{3,27},{28,4},{13,5},{6,14},{23,15},{40,48}... | collective-permute-start | bytes 1966088 | tf_op jit(solution)/shard_map/ppermute | solution.py:292
  378.0 30.5 %all-to-all-start.4 = ((f32[64,32,256]{2,1,0:T(8,128)}), f32[64,32,256]{2,1,0:T(8,128)}, u32[]{:S(2)}, u32[]{:S(2)}) async-start(f32[64,32,256]{2,1,0:T(8,128)} %get-tuple-element.30), calls=%async_computation.4 | async-start | bytes 4194304 | tf_op jit(solution)/shard_map/all_to_all | solution.py:363
  393.8 25.7 %collective-permute-start.11 = (f32[10,64,512]{2,1,0:T(8,128)S(1)}, f32[10,64,512]{2,1,0:T(8,128)}, u32[]{:S(2)}, u32[]{:S(2)}) collective-permute-start(f32[10,64,512]{2,1,0:T(8,128)S(1)} %slab_strip.7), channel_id=1, source_target_pairs={{0,2},{8,10},{16,18},{24,26},{32,34},{40,42},{48,50},{56,58},{64,6... | collective-permute-start | bytes 3932168 | tf_op jit(solution)/shard_map/ppermute | solution.py:272
  401.1 25.6 %collective-permute-start.24 = (f32[10,32,512]{2,1,0:T(8,128)}, f32[10,32,512]{2,1,0:T(8,128)}, u32[]{:S(2)}, u32[]{:S(2)}) collective-permute-start(f32[10,32,512]{2,1,0:T(8,128)} %slab_strip.9), channel_id=1, source_target_pairs={{0,4},{8,12},{16,20},{24,28},{32,36},{40,44},{48,52},{56,60},{64,6... | collective-permute-start | bytes 1966088 | tf_op jit(solution)/shard_map/ppermute | solution.py:272
  405.5 28.2 %collective-permute-start.22 = (f32[10,32,512]{2,1,0:T(8,128)}, f32[10,32,512]{2,1,0:T(8,128)}, u32[]{:S(2)}, u32[]{:S(2)}) collective-permute-start(f32[10,32,512]{2,1,0:T(8,128)} %slab_strip.9), channel_id=1, source_target_pairs={{0,2},{8,10},{16,18},{24,26},{32,34},{40,42},{48,50},{56,58},{64,6... | collective-permute-start | bytes 1966088 | tf_op jit(solution)/shard_map/ppermute | solution.py:272
  413.2 27.3 %collective-permute-start.17 = (f32[10,32,512]{2,1,0:T(8,128)S(1)}, f32[10,32,512]{2,1,0:T(8,128)}, u32[]{:S(2)}, u32[]{:S(2)}) collective-permute-start(f32[10,32,512]{2,1,0:T(8,128)S(1)} %slab_strip.8), channel_id=1, source_target_pairs={{0,4},{8,12},{16,20},{24,28},{32,36},{40,44},{48,52},{56,60},{64,6... | collective-permute-start | bytes 1966088 | tf_op jit(solution)/shard_map/ppermute | solution.py:272
  455.6 26.0 %collective-permute-start.34 = (f32[5,32,512]{2,1,0:T(8,128)S(1)}, f32[5,32,512]{2,1,0:T(8,128)}, u32[]{:S(2)}, u32[]{:S(2)}) collective-permute-start(f32[5,32,512]{2,1,0:T(8,128)S(1)} %select_select_fusion.3), channel_id=1, source_target_pairs={{8,16},{25,17},{18,26},{3,27},{28,4},{13,5},{6,14},{23,15},{40,48}... | collective-permute-start | bytes 983048 | tf_op jit(solution)/shard_map/ppermute | solution.py:292
  457.2 36.0 %collective-permute-start.28 = (f32[5,64,512]{2,1,0:T(8,128)S(1)}, f32[5,64,512]{2,1,0:T(8,128)}, u32[]{:S(2)}, u32[]{:S(2)}) collective-permute-start(f32[5,64,512]{2,1,0:T(8,128)S(1)} %select_select_fusion), channel_id=1, source_target_pairs={{8,16},{25,17},{18,26},{3,27},{28,4},{13,5},{6,14},{23,15},{40,48}... | collective-permute-start | bytes 1966088 | tf_op jit(solution)/shard_map/ppermute | solution.py:292
  458.8 33.4 %collective-permute-start.31 = (f32[5,32,512]{2,1,0:T(8,128)S(1)}, f32[5,32,512]{2,1,0:T(8,128)}, u32[]{:S(2)}, u32[]{:S(2)}) collective-permute-start(f32[5,32,512]{2,1,0:T(8,128)S(1)} %select_select_fusion.4), channel_id=1, source_target_pairs={{8,16},{25,17},{18,26},{3,27},{28,4},{13,5},{6,14},{23,15},{40,48}... | collective-permute-start | bytes 983048 | tf_op jit(solution)/shard_map/ppermute | solution.py:292
  (48 other events, 606.9 us)
Sparse Core Ops, SparseCore 0:
  9.6 46.8 all-gather.3
  58.2 37.2 all-gather.5

commit v3 on v2

v3 whole, which is shorter than its diff:
```python
import jax
import jax.numpy as jnp
from jax import lax
from jax.experimental import pallas as pl
from jax.experimental.pallas import tpu as pltpu
from jax.sharding import PartitionSpec as P

ORDER = 10240
BS = 256
CAP = 4
PIV = 512
STRIP = 32
NSTRIP = BS // STRIP
PARTS = (2, 3, 3)
OFFSETS = tuple(sum(PARTS[:q]) for q in range(len(PARTS)))
NPART = len(PARTS)
GROUP = 8
RING = 8

HIGH = lax.Precision.HIGHEST
f32, bf16, i32 = jnp.float32, jnp.bfloat16, jnp.int32


def lower_sym(block):
    return jnp.tril(block) + jnp.tril(block, -1).T


def permute_kernel(slot_ref, tile_ref, rows_ref, cols_ref, *refs):
    strip_refs, part_refs = refs[:NSTRIP], refs[NSTRIP : NSTRIP + NPART]
    hold, strip_sems, part_sems = refs[NSTRIP + NPART :]
    step = pl.program_id(0)
    half = BS // 2
    lane = lax.broadcasted_iota(i32, (BS, half), 1)
    place = lax.broadcasted_iota(i32, (BS, BS), 0)

    def move(g, carry):
        t = step * GROUP + g
        tile = tile_ref[g]
        high = tile.astype(bf16)
        rest = tile - high.astype(f32)
        mid = rest.astype(bf16)
        low = (rest - mid.astype(f32)).astype(bf16)
        parts = jnp.concatenate([high, mid, low], axis=1)
        wanted = jnp.transpose(jnp.broadcast_to(rows_ref[g], (half, BS)))
        pick_rows = jnp.concatenate(
            [jnp.where(wanted == lane + k * half, 1.0, 0.0) for k in range(2)], axis=1
        ).astype(bf16)
        pick_cols = jnp.where(place == cols_ref[g], 1.0, 0.0).astype(bf16)
        moved = jnp.dot(pick_rows, parts, preferred_element_type=f32).astype(bf16)
        out = jnp.dot(moved[:, :BS], pick_cols, preferred_element_type=f32)
        out = out + jnp.dot(moved[:, BS : 2 * BS], pick_cols, preferred_element_type=f32)
        out = out + jnp.dot(moved[:, 2 * BS :], pick_cols, preferred_element_type=f32)
        hold[t] = out.reshape(NSTRIP, STRIP, BS)
        for k in range(NSTRIP):
            pltpu.make_async_copy(hold.at[t, k], strip_refs[k].at[t], strip_sems.at[t]).start()
        for q in range(NPART):
            pltpu.make_async_copy(
                hold.at[t, pl.ds(OFFSETS[q], PARTS[q])],
                part_refs[q].at[slot_ref[t]],
                part_sems.at[t],
            ).start()
        return carry

    lax.fori_loop(0, GROUP, move, 0, unroll=2)

    @pl.when(step == pl.num_programs(0) - 1)
    def _():
        def finish(t, carry):
            pltpu.make_async_copy(hold.at[t], hold.at[t], strip_sems.at[t]).wait()
            pltpu.make_async_copy(hold.at[t], hold.at[t], part_sems.at[t]).wait()
            return carry

        lax.fori_loop(0, hold.shape[0], finish, 0)


def permute(slot, tiles, rows_from, cols_from, slots):
    count = tiles.shape[0]
    out = pl.pallas_call(
        permute_kernel,
        grid_spec=pltpu.PrefetchScalarGridSpec(
            num_scalar_prefetch=1,
            grid=(count // GROUP,),
            in_specs=[
                pl.BlockSpec((GROUP, BS, BS), lambda t, slot: (t, 0, 0)),
                pl.BlockSpec((GROUP, 1, BS), lambda t, slot: (t, 0, 0)),
                pl.BlockSpec((GROUP, 1, BS), lambda t, slot: (t, 0, 0)),
            ],
            out_specs=[pl.BlockSpec(memory_space=pl.ANY)] * (NSTRIP + NPART),
            scratch_shapes=[
                pltpu.VMEM((count, NSTRIP, STRIP, BS), f32),
                pltpu.SemaphoreType.DMA((count,)),
                pltpu.SemaphoreType.DMA((count,)),
            ],
        ),
        out_shape=[jax.ShapeDtypeStruct((count, STRIP, BS), f32)] * NSTRIP
        + [jax.ShapeDtypeStruct((slots, n, STRIP, BS), f32) for n in PARTS],
        compiler_params=pltpu.CompilerParams(vmem_limit_bytes=58 << 20),
        cost_estimate=pl.CostEstimate(
            flops=12 * count * BS**3, bytes_accessed=12 * count * BS * BS, transcendentals=0
        ),
        name="permute_tiles",
    )(slot, tiles, rows_from[:, None, :], cols_from[:, None, :])
    return out[:NSTRIP], out[NSTRIP:]


def slot_kernel(count, meta, *refs):
    sources, (out_ref, sems) = refs[:NSTRIP], refs[NSTRIP:]
    for c in range(NSTRIP):

        @pl.when(meta[count] == c)
        def _():
            def begin(t, carry):
                pltpu.make_async_copy(sources[c].at[t], out_ref.at[meta[t]], sems.at[t]).start()
                return carry

            lax.fori_loop(0, count, begin, 0)

    def finish(t, carry):
        pltpu.make_async_copy(sources[0].at[t], out_ref.at[meta[t]], sems.at[t]).wait()
        return carry

    lax.fori_loop(0, count, finish, 0)


def slot_strips(meta, sources, slots):
    count = sources[0].shape[0]
    return pl.pallas_call(
        lambda *refs: slot_kernel(count, *refs),
        grid_spec=pltpu.PrefetchScalarGridSpec(
            num_scalar_prefetch=1,
            grid=(1,),
            in_specs=[pl.BlockSpec(memory_space=pl.ANY)] * NSTRIP,
            out_specs=pl.BlockSpec(memory_space=pl.ANY),
            scratch_shapes=[pltpu.SemaphoreType.DMA((count,))],
        ),
        out_shape=jax.ShapeDtypeStruct((slots, STRIP, BS), f32),
        compiler_params=pltpu.CompilerParams(vmem_limit_bytes=58 << 20),
        cost_estimate=pl.CostEstimate(
            flops=0, bytes_accessed=8 * count * STRIP * BS, transcendentals=0
        ),
        name="slot_strips",
    )(meta, *sources)


def slab_kernel(meta, initial_ref, in_ref, out_ref, ring, sems):
    total = meta[128]

    def copy(g):
        return pltpu.make_async_copy(in_ref.at[meta[g]], ring.at[g % RING], sems.at[g % RING])

    for g in range(RING):

        @pl.when(g < total)
        def _():
            copy(g).start()

    out_ref[...] = initial_ref[...]

    @pl.loop(0, total)
    def _(g):
        copy(g).wait()
        spot = meta[64 + g]
        cols = pl.ds(pl.multiple_of((spot % 2) * BS, BS), BS)
        out_ref[spot // 2, :, cols] += ring[g % RING]

        @pl.when(g + RING < total)
        def _():
            copy(g + RING).start()


def slab_strip(meta, initial, incoming):
    spec = pl.BlockSpec(initial.shape, lambda i, meta: (0, 0, 0))
    return pl.pallas_call(
        slab_kernel,
        grid_spec=pltpu.PrefetchScalarGridSpec(
            num_scalar_prefetch=1,
            grid=(1,),
            in_specs=[spec, pl.BlockSpec(memory_space=pl.ANY)],
            out_specs=spec,
            scratch_shapes=[
                pltpu.VMEM((RING, STRIP, BS), f32),
                pltpu.SemaphoreType.DMA((RING,)),
            ],
        ),
        out_shape=jax.ShapeDtypeStruct(initial.shape, f32),
        compiler_params=pltpu.CompilerParams(vmem_limit_bytes=32 << 20),
        cost_estimate=pl.CostEstimate(
            flops=0, bytes_accessed=12 * initial.size, transcendentals=0
        ),
        name="slab_strip",
    )(meta, initial, incoming)


def halves(x):
    high = x.astype(bf16)
    return high, (x - high.astype(f32)).astype(bf16)


def nt(a, b):
    return lax.dot_general(a, b, (((1,), (1,)), ((), ())), preferred_element_type=f32)


def final_kernel(col_blocks, *refs):
    meta = refs[0]
    slab, across, first_inv, second_inv, cross, first_factor, second_factor = refs[1:8]
    incoming = refs[8 : 8 + NPART]
    out_ref, a_high, a_low, ring, sems = refs[8 + NPART :]
    b = pl.program_id(0)
    total = meta[138]

    def copies(g):
        return [
            pltpu.make_async_copy(
                incoming[q].at[meta[g]],
                ring.at[g % RING, pl.ds(OFFSETS[q], PARTS[q])],
                sems.at[g % RING, q],
            )
            for q in range(NPART)
        ]

    def solve(block, keep_first, keep_second):
        one = jnp.dot(block[:, :BS], first_inv[...], precision=HIGH, preferred_element_type=f32)
        one = jnp.where(keep_first == 1, one, 0.0)
        two = jnp.dot(block[:, BS:], second_inv[...], precision=HIGH, preferred_element_type=f32)
        two = two - jnp.dot(one, cross[...], precision=HIGH, preferred_element_type=f32)
        return one, jnp.where(keep_second == 1, two, 0.0)

    @pl.when(b == 0)
    def _():
        for g in range(RING):

            @pl.when(g < total)
            def _():
                for c in copies(g):
                    c.start()

        for cb in range(col_blocks):
            block = across[:, cb].reshape(BS, PIV)
            one, two = solve(block, meta[159 + cb], meta[164 + cb])
            high, low = halves(jnp.concatenate([one, two], axis=1))
            a_high[cb * BS : (cb + 1) * BS] = high
            a_low[cb * BS : (cb + 1) * BS] = low

    one, two = solve(slab[:, 0].reshape(BS, PIV), meta[139 + b], meta[149 + b])
    top = meta[169] == 1
    high, low = halves(
        jnp.where(jnp.logical_and(top, b < 2), 0.0, jnp.concatenate([one, two], axis=1))
    )
    for cb in range(col_blocks):
        rows = slice(cb * BS, (cb + 1) * BS)
        product = nt(high, a_high[rows]) + (nt(high, a_low[rows]) + nt(low, a_high[rows]))
        out_ref[:, rows] = -product

    @pl.loop(meta[128 + b], meta[129 + b])
    def _(g):
        for c in copies(g):
            c.wait()
        cols = pl.ds(pl.multiple_of(meta[64 + g] * BS, BS), BS)
        out_ref[:, cols] += ring[g % RING].reshape(BS, BS)

        @pl.when(g + RING < total)
        def _():
            for c in copies(g + RING):
                c.start()

    @pl.when(meta[170] == 1)
    def _():
        out_ref[:, :BS] = jnp.where(jnp.logical_and(top, b == 0), first_factor[...], one)
        out_ref[:, BS:PIV] = jnp.where(jnp.logical_and(top, b == 1), second_factor[...], two)


def final(meta, slab, across, mats, incoming, row_blocks, col_blocks):
    whole = pl.BlockSpec((BS, BS), lambda b, meta: (0, 0))
    return pl.pallas_call(
        lambda *refs: final_kernel(col_blocks, *refs),
        grid_spec=pltpu.PrefetchScalarGridSpec(
            num_scalar_prefetch=1,
            grid=(row_blocks,),
            in_specs=[
                pl.BlockSpec((NSTRIP, 1, STRIP, PIV), lambda b, meta: (0, b, 0, 0)),
                pl.BlockSpec((NSTRIP, col_blocks, STRIP, PIV), lambda b, meta: (0, 0, 0, 0)),
            ]
            + [whole] * 5
            + [pl.BlockSpec(memory_space=pl.ANY)] * NPART,
            out_specs=pl.BlockSpec((BS, col_blocks * BS), lambda b, meta: (b, 0)),
            scratch_shapes=[
                pltpu.VMEM((col_blocks * BS, PIV), bf16),
                pltpu.VMEM((col_blocks * BS, PIV), bf16),
                pltpu.VMEM((RING, NSTRIP, STRIP, BS), f32),
                pltpu.SemaphoreType.DMA((RING, NPART)),
            ],
        ),
        out_shape=jax.ShapeDtypeStruct((row_blocks * BS, col_blocks * BS), f32),
        compiler_params=pltpu.CompilerParams(vmem_limit_bytes=48 << 20),
        cost_estimate=pl.CostEstimate(
            flops=6 * row_blocks * col_blocks * BS * BS * PIV,
            bytes_accessed=4 * 2 * row_blocks * col_blocks * BS * BS,
            transcendentals=0,
        ),
        name="place_and_update",
    )(meta, slab, across, *mats, *incoming)


def dot(a, b):
    return jnp.dot(a, b, precision=HIGH)


def inverse(lower):
    size = lower.shape[0]
    eye = jnp.eye(size, dtype=f32)
    scale = jnp.sum(lower * eye, axis=0)
    power = eye - lower / scale[None, :]
    out = eye + power
    for _ in range(6):
        power = dot(power, power)
        out = out + dot(power, out)
    return out / scale[:, None]


def panel(block):
    half = BS // 2
    first = jnp.linalg.cholesky(lower_sym(block[:half, :half]))
    first_inv = inverse(first)
    below = dot(block[half:, :half], first_inv.T)
    second = jnp.linalg.cholesky(lower_sym(block[half:, half:] - dot(below, below.T)))
    second_inv = inverse(second)
    across = -dot(second_inv, dot(below, first_inv))
    zero = jnp.zeros((half, half), f32)
    factor = jnp.block([[first, zero], [below, second]])
    return factor, jnp.block([[first_inv.T, across.T], [zero, second_inv.T]])


def ordered(key, valid, span):
    count = key.shape[0]
    key = jnp.where(valid, key, span)
    index = jnp.arange(count, dtype=i32)
    ahead = (key[None, :] < key[:, None]) | (
        (key[None, :] == key[:, None]) & (index[None, :] < index[:, None])
    )
    rank = jnp.sum(ahead.astype(i32), axis=1)
    chosen = rank[None, :] == index[:, None]
    order = jnp.sum(jnp.where(chosen, index[None, :], 0), axis=1)
    return order, jnp.sum(jnp.where(chosen, key[None, :], 0), axis=1), key


def body(tiles, dest, block_row, block_col, rows_from, cols_from, initial, pattern):
    n_front = lax.axis_size("front")
    n_row = lax.axis_size("row")
    n_col = lax.axis_size("col")
    my_row = lax.axis_index("row")
    my_col = lax.axis_index("col")
    row_blocks = ORDER // n_row // BS
    col_blocks = ORDER // n_col // BS
    lead = PIV // BS
    slots = n_front * n_row * CAP
    target = dest[:, 0]
    owner_row = target % n_row
    local_row = jnp.where(owner_row == 0, lead + block_row % (row_blocks - lead), block_row)
    block_id = local_row * col_blocks + block_col
    same = (target[:, None] == target[None, :]).astype(i32)
    slot = target * CAP + jnp.sum(jnp.tril(same, -1), axis=1)
    choose = jnp.arange(slots, dtype=i32)[:, None] == slot[None, :]
    labels = jnp.where(
        jnp.any(choose, axis=1), jnp.sum(jnp.where(choose, block_id[None, :], 0), axis=1), -1
    )
    names = lax.all_to_all(labels, ("front", "row"), split_axis=0, concat_axis=0, tiled=True)

    row = jnp.zeros((1, initial.shape[2]), f32)
    slot_row = row.at[0, : slot.shape[0]].set(slot.astype(f32))
    near = lax.all_gather(
        jnp.concatenate([initial[0, :PIV], jnp.broadcast_to(slot_row, (8, row.shape[1]))]),
        ("row", "col"),
        axis=0,
    )
    corner = near[:n_col, :PIV].transpose(1, 0, 2).reshape(PIV, PIV)
    first_slot = lax.dynamic_index_in_dim(near[:, PIV], my_row * n_col, 0, keepdims=False)
    slot_meta = jnp.append(first_slot[: slot.shape[0]].astype(i32), my_col)
    names_row = row.at[0, :slots].set(names.astype(f32))
    wide = lax.all_gather(
        jnp.concatenate([initial[0], jnp.broadcast_to(names_row, (8, row.shape[1]))]), "col", axis=0
    )
    first_names = wide[0, row_blocks * BS, :slots].astype(i32)
    columns = wide[:, : row_blocks * BS].reshape(n_col, row_blocks, NSTRIP, STRIP, -1)
    columns = lax.dynamic_index_in_dim(columns, my_col, 2, keepdims=False)
    columns = columns.transpose(1, 2, 0, 3).reshape(row_blocks, STRIP, PIV)

    valid = names >= 0
    order, sorted_id, key = ordered(names, valid, row_blocks * col_blocks)
    bounds = jnp.arange(row_blocks + 1, dtype=i32)[:, None] * col_blocks
    starts = jnp.sum((key[None, :] < bounds).astype(i32), axis=1)
    in_slab = (first_names >= 0) & (first_names % col_blocks < lead)
    slab_key = (first_names // col_blocks) * lead + first_names % col_blocks
    slab_order, slab_id, _ = ordered(slab_key, in_slab, row_blocks * lead)
    slab_meta = jnp.concatenate([slab_order, slab_id, jnp.sum(in_slab.astype(i32))[None]])

    def kept(first_block, count):
        blocks = first_block + jnp.arange(count, dtype=i32)
        flags = lax.dynamic_slice_in_dim(pattern[0], first_block, count, axis=1)
        ahead = blocks[None, :] > jnp.arange(2, dtype=i32)[:, None]
        return jnp.where(ahead, flags, 0).reshape(-1)

    meta = jnp.concatenate(
        [
            order,
            sorted_id % col_blocks,
            starts,
            kept(my_row * row_blocks, row_blocks),
            kept(my_col * col_blocks, col_blocks),
            (my_row == 0).astype(i32)[None],
            (my_col == 0).astype(i32)[None],
        ]
    )

    def send(part):
        return lax.all_to_all(part, ("front", "row"), split_axis=0, concat_axis=0, tiled=True)

    strips, parts = permute(slot, tiles, rows_from, cols_from, slots)
    incoming = [send(parts[0])]
    sources = [strips[0]] + [lax.ppermute(strips[c], "col", [(0, c)]) for c in range(1, n_col)]
    strip = slab_strip(slab_meta, columns, send(slot_strips(slot_meta, sources, slots)))

    first, first_inv = panel(corner[:BS, :BS])
    below = dot(corner[BS:, :BS], first_inv)
    below = jnp.where(pattern[0, 0, 1] == 1, below, jnp.zeros_like(below))
    second, second_inv = panel(corner[BS:, BS:] - dot(below, below.T))
    mats = (first_inv, second_inv, dot(below.T, second_inv), first, second)

    part, strip = lax.optimization_barrier((parts[1], strip))
    incoming.append(send(part))
    slab = lax.all_gather(strip, "col", axis=0)
    own = lax.dynamic_slice_in_dim(slab, (my_col % 2) * col_blocks, col_blocks, 1)
    own = jnp.where(my_row == my_col // 2, own, jnp.zeros_like(own))
    part, own, mats = lax.optimization_barrier((parts[2], own, mats))
    incoming.append(send(part))
    across = lax.psum(own, "row")
    return final(meta, slab, across, mats, incoming, row_blocks, col_blocks)[None]


def solution(mesh):
    placed = (
        P(("front", "row", "col"), None, None),
        P(("front", "row", "col"), None),
        P(("front", "row", "col")),
        P(("front", "row", "col")),
        P(("front", "row", "col"), None),
        P(("front", "row", "col"), None),
        P("front", "row", "col"),
        P("front", None, None),
    )
    return jax.shard_map(
        body, mesh=mesh, in_specs=placed, out_specs=P("front", "row", "col"), check_vma=False
    )
```

time: 545 us -> 519 us (0.952)
  the two profiles are of different devices: /device:TPU:64 before, /device:TPU:7 now
where the time goes in v3:
time: 519 us; the launch traced here: 510 us
  waiting for transfers between devices  241 us (46%)
  Pallas kernels  85.4 us (16%)
  other arithmetic  70.3 us (14%)
  starting transfers between devices  51.5 us (10%)
  local copies, waits for them, and re-layouts  31.5 us (6%)
  matrix products  15.3 us (3%)
  between operations  15 us (3%)
    psum x1, waiting for transfers between devices, body(): across = lax.psum(own, 'row')  176 us
    all_to_all x4, waiting for transfers between devices, send(): lax.all_to_all(part, ('front', 'row'), split_axis=0, concat_axis=0, tiled...  48.8 us
    pallas_call x1, Pallas kernels, slot_strips(): pl.pallas_call(lambda *refs: slot_kernel(count, *refs), grid_spec=pltpu.P...  33.8 us
    pallas_call x1, Pallas kernels, final(): pl.pallas_call(lambda *refs: final_kernel(col_blocks, *refs), grid_spec=p...  32.5 us
    all_to_all x4, starting transfers between devices, send(): lax.all_to_all(part, ('front', 'row'), split_axis=0, concat_axis=0, tiled...  31.8 us
    another operation x6, other arithmetic, panel(): jnp.linalg.cholesky(lower_sym(block[half:, half:] - dot(below, below.T)))  24.8 us
    another operation x6, other arithmetic, panel(): first = jnp.linalg.cholesky(lower_sym(block[:half, :half]))  24.8 us
    pallas_call x1, Pallas kernels, permute(): pl.pallas_call(permute_kernel, grid_spec=pltpu.PrefetchScalarGridSpec(num...  16.5 us
  transfers between devices with their start and end apart: 16, of which 6 were waited for; matrix products, arithmetic and copies ran while one was open for 22% of the time, Pallas kernels for 10%

profile of v3, /device:TPU:7, one launch (start us, length us, event | category | flops | bytes accessed | tf_op | source)
XLA Modules:
  0.0 510.4 jit_solution(14481841741230914837)
XLA Ops:
  12.7 7.7 %all-to-all-start = ((s32[16,4,1]{1,2,0:T(1,128)}), s32[16,4,1]{1,2,0:T(1,128)S(1)}, u32[]{:S(2)}, u32[]{:S(2)}) async-start(s32[16,4,1]{1,2,0:T(1,128)} %bitcast.1), calls=%async_computation | async-start | bytes 16384 | tf_op jit(solution)/shard_map/all_to_all | solution.py:366
  27.0 2.0 maximum_bitcast_fusion
  29.1 16.5 %permute_tiles.1 = (f32[32,32,256]{2,1,0:T(8,128)}, f32[32,32,256]{2,1,0:T(8,128)}, f32[32,32,256]{2,1,0:T(8,128)}, f32[32,32,256]{2,1,0:T(8,128)}, f32[32,32,25...) custom-call(s32[32]{0:T(128)} %copy-done.8, ...), custom_call_target="tpu_custom_call" | custom-call | flops 6442450944 | bytes 25165824 | tf_op jit(solution)/shard_map/permute_tiles/pallas_call | solution.py:78
  55.6 6.2 %all-gather.13.cloned.1.call-done = f32[32,520,64]{1,2,0:T(8,128)} async-done(((f32[1,520,64]{1,2,0:T(8,128)}), f32[32,520,64]{1,2,0:T(8,128)}) %all-gather.13.cloned.1.call-update) | async-done | bytes 4259856 | tf_op jit(solution)/shard_map/all_gather | solution.py:370
  63.5 11.7 %cholesky.74 = f32[128,128]{1,0:T(8,128)S(1)} custom-call(f32[128,128]{1,0:T(8,128)S(1)} %copy.166), custom_call_target="Cholesky" | custom-call | tf_op jit(solution)/shard_map/jit(cholesky)/cholesky | solution.py:322
  80.5 2.1 collective-permute-start.6
  86.7 11.7 %cholesky.85 = f32[128,128]{1,0:T(8,128)S(1)} custom-call(f32[128,128]{1,0:T(8,128)S(1)} %copy.171), custom_call_target="Cholesky" | custom-call | tf_op jit(solution)/shard_map/jit(cholesky)/cholesky | solution.py:325
  99.2 33.8 %slot_strips.1 = f32[64,32,256]{2,1,0:T(8,128)} custom-call(s32[33]{0:T(128)} %pad_add_fusion.1.refs_0_, f32[32,32,256]{2,1,0:T(8,128)} %get-tuple-element.51.refs_1_, f32[32,32,256]{2,1,0:T(8,128)} %copy-done.2, f32[32,32,256]{2,1,0:T(8,128)} %collective-permute-done.1.refs_3_, f32[32,32,256]{2,1,0:T(8,128)} %collective-permute-done.2.refs_4_, ...), custom_call_target="tpu_custom_call" | custom-call | bytes 2097152 | tf_op jit(solution)/shard_map/slot_strips/pallas_call | solution.py:127
  133.1 6.3 %all-to-all-start.1 = ((f32[64,32,256]{2,1,0:T(8,128)}), f32[64,32,256]{2,1,0:T(8,128)S(1)}, u32[]{:S(2)}, u32[]{:S(2)}) async-start(f32[64,32,256]{2,1,0:T(8,128)} %slot_strips.1), calls=%async_computation.1 | async-start | bytes 4194304 | tf_op jit(solution)/shard_map/all_to_all | solution.py:415
  143.9 5.1 slice.100
  149.0 8.4 %copy.214 = f32[8,2560,64]{2,1,0:T(8,128)} copy(f32[8,2560,64]{1,2,0:T(8,128)} %slice.100) | data formatting | bytes 10485760
  158.9 1.9 copy.162
  164.2 6.7 %all-to-all-start.2 = ((f32[64,2,32,256]{3,2,1,0:T(8,128)}), f32[64,2,32,256]{3,2,1,0:T(8,128)}, u32[]{:S(2)}, u32[]{:S(2)}) async-start(f32[64,2,32,256]{3,2,1,0:T(8,128)} %get-tuple-element.67), calls=%async_computation.2 | async-start | bytes 8388608 | tf_op jit(solution)/shard_map/all_to_all | solution.py:415
  172.6 2.6 slab_strip.1
  178.4 11.7 %cholesky.96 = f32[128,128]{1,0:T(8,128)S(1)} custom-call(f32[128,128]{1,0:T(8,128)S(1)} %copy.182), custom_call_target="Cholesky" | custom-call | tf_op jit(solution)/shard_map/jit(cholesky)/cholesky | solution.py:322
  193.5 13.5 %all-to-all-done.2.refs_8_ = f32[64,2,32,256]{3,2,1,0:T(8,128)} async-done(((f32[64,2,32,256]{3,2,1,0:T(8,128)}), f32[64,2,32,256]{3,2,1,0:T(8,128)}, u32[]{:S(2)}, u32[]{:S(2)}) %all-to-all-start.2) | async-done | bytes 4194336 | tf_op jit(solution)/shard_map/all_to_all | solution.py:415
  207.0 9.3 %all-to-all-start.3 = ((f32[64,3,32,256]{3,2,1,0:T(8,128)}), f32[64,3,32,256]{3,2,1,0:T(8,128)}, u32[]{:S(2)}, u32[]{:S(2)}) async-start(f32[64,3,32,256]{3,2,1,0:T(8,128)} %get-tuple-element.68), calls=%async_computation.3 | async-start | bytes 12582912 | tf_op jit(solution)/shard_map/all_to_all | solution.py:415
  217.8 11.7 %cholesky.107 = f32[128,128]{1,0:T(8,128)S(1)} custom-call(f32[128,128]{1,0:T(8,128)S(1)} %fusion.9), custom_call_target="Cholesky" | custom-call | tf_op jit(solution)/shard_map/jit(cholesky)/cholesky | solution.py:325
  234.7 8.6 %all-gather.9.cloned.1.call-done = f32[80,32,512]{2,1,0:T(8,128)} async-done(((f32[10,32,512]{2,1,0:T(8,128)}), f32[80,32,512]{2,1,0:T(8,128)}) %all-gather.9.cloned.1.call-update) | async-done | bytes 5242896 | tf_op jit(solution)/shard_map/all_gather | solution.py:430
  243.3 3.7 dynamic-slice_select_fusion
  247.0 35.3 %all-to-all-done.3.refs_9_ = f32[64,3,32,256]{3,2,1,0:T(8,128)} async-done(((f32[64,3,32,256]{3,2,1,0:T(8,128)}), f32[64,3,32,256]{3,2,1,0:T(8,128)}, u32[]{:S(2)}, u32[]{:S(2)}) %all-to-all-start.3) | async-done | bytes 6291488 | tf_op jit(solution)/shard_map/all_to_all | solution.py:415
  282.4 9.4 %all-to-all-start.4 = ((f32[64,3,32,256]{3,2,1,0:T(8,128)}), f32[64,3,32,256]{3,2,1,0:T(8,128)}, u32[]{:S(2)}, u32[]{:S(2)}) async-start(f32[64,3,32,256]{3,2,1,0:T(8,128)} %get-tuple-element.69), calls=%async_computation.4 | async-start | bytes 12582912 | tf_op jit(solution)/shard_map/all_to_all | solution.py:415
  293.8 175.5 %all-reduce.7.cloned.1.call-done.refs_2_ = f32[8,5,32,512]{3,2,1,0:T(8,128)} async-done(((f32[8,5,32,512]{3,2,1,0:T(8,128)}), f32[8,5,32,512]{3,2,1,0:T(8,128)}) %all-reduce.7.cloned.1.call-update) | async-done | bytes 2621456 | tf_op jit(solution)/shard_map/psum | solution.py:435
  471.1 32.5 %place_and_update.1 = f32[2560,1280]{1,0:T(8,128)} custom-call(s32[171]{0:T(256)S(1)} %concatenate.59.refs_0_, f32[8,10,32,512]{3,2,1,0:T(8,128)} %bitcast.161, f32[8,5,32,512]{3,2,1,0:T(8,128)S(1)} %copy-done, f32[256,256]{1,0:T(8,128)S(1)} %copy.197.refs_3_, f32[256,256]{1,0:T(8,128)S(1)} %copy.198.refs_4_, f32[256,256]{1,0:T(8,128)S(1)} %fusion.30.refs_5_, ...), custom_call_target="tpu_custom_call" | custom-call | flops 10066329600 | bytes 26214400 | tf_op jit(solution)/shard_map/place_and_update/pallas_call | solution.py:274
  (200 shorter events, 61.2 us)
Async XLA Ops:
  6.5 55.2 %all-gather.13.cloned.1.call-start = ((), (), s32[]{:S(2)}) async-start(), calls=%async_computation.8 | async-start | bytes 5406720 | tf_op jit(solution)/shard_map/all_gather | solution.py:370
  10.3 18.7 %copy-start.8 = (s32[32]{0:T(128)}, s32[32]{0:T(128)S(1)}, u32[]{:S(2)}) copy-start(s32[32]{0:T(128)S(1)} %get-tuple-element.87.slot_ref) | copy-start | bytes 388
  12.7 12.3 %all-to-all-start = ((s32[16,4,1]{1,2,0:T(1,128)}), s32[16,4,1]{1,2,0:T(1,128)S(1)}, u32[]{:S(2)}, u32[]{:S(2)}) async-start(s32[16,4,1]{1,2,0:T(1,128)} %bitcast.1), calls=%async_computation | async-start | bytes 16384 | tf_op jit(solution)/shard_map/all_to_all | solution.py:366
  20.4 123.5 %all-gather.11.cloned.1.call-start = ((), (), s32[]{:S(2)}) async-start(), calls=%async_computation.7 | async-start | bytes 6193152 | tf_op jit(solution)/shard_map/all_gather | solution.py:379
  29.1 24.4 %copy-start.6 = (s32[1,2,40]{2,1,0:T(2,128)S(1)}, s32[1,2,40]{2,1,0:T(2,128)}, u32[]{:S(2)}) copy-start(s32[1,2,40]{2,1,0:T(2,128)} %param.20) | copy-start | bytes 964
  45.6 33.3 %collective-permute-start = (f32[32,32,256]{2,1,0:T(8,128)}, f32[32,32,256]{2,1,0:T(8,128)S(1)}, u32[]{:S(2)}, u32[]{:S(2)}) collective-permute-start(f32[32,32,256]{2,1,0:T(8,128)} %get-tuple-element.52), channel_id=1, source_target_pairs={{0,1},{8,9},{16,17},{24,25},{32,33},{40,41},{48,49},{56,57},{64,65... | collective-permute-start | bytes 3145736 | tf_op jit(solution)/shard_map/ppermute | solution.py:419
  46.9 33.7 %collective-permute-start.1 = (f32[32,32,256]{2,1,0:T(8,128)}, f32[32,32,256]{2,1,0:T(8,128)}, u32[]{:S(2)}, u32[]{:S(2)}) collective-permute-start(f32[32,32,256]{2,1,0:T(8,128)} %get-tuple-element.53), channel_id=1, source_target_pairs={{0,2},{8,10},{16,18},{24,26},{32,34},{40,42},{48,50},{56,58},{64,6... | collective-permute-start | bytes 3145736 | tf_op jit(solution)/shard_map/ppermute | solution.py:419
  48.5 50.7 %collective-permute-start.2 = (f32[32,32,256]{2,1,0:T(8,128)}, f32[32,32,256]{2,1,0:T(8,128)}, u32[]{:S(2)}, u32[]{:S(2)}) collective-permute-start(f32[32,32,256]{2,1,0:T(8,128)} %get-tuple-element.54), channel_id=1, source_target_pairs={{0,3},{8,11},{16,19},{24,27},{32,35},{40,43},{48,51},{56,59},{64,6... | collective-permute-start | bytes 3145736 | tf_op jit(solution)/shard_map/ppermute | solution.py:419
  50.2 49.0 %collective-permute-start.3 = (f32[32,32,256]{2,1,0:T(8,128)}, f32[32,32,256]{2,1,0:T(8,128)}, u32[]{:S(2)}, u32[]{:S(2)}) collective-permute-start(f32[32,32,256]{2,1,0:T(8,128)} %get-tuple-element.55), channel_id=1, source_target_pairs={{0,4},{8,12},{16,20},{24,28},{32,36},{40,44},{48,52},{56,60},{64,6... | collective-permute-start | bytes 3145736 | tf_op jit(solution)/shard_map/ppermute | solution.py:419
  51.8 47.4 %collective-permute-start.4 = (f32[32,32,256]{2,1,0:T(8,128)}, f32[32,32,256]{2,1,0:T(8,128)}, u32[]{:S(2)}, u32[]{:S(2)}) collective-permute-start(f32[32,32,256]{2,1,0:T(8,128)} %get-tuple-element.56), channel_id=1, source_target_pairs={{0,5},{8,13},{16,21},{24,29},{32,37},{40,45},{48,53},{56,61},{64,6... | collective-permute-start | bytes 3145736 | tf_op jit(solution)/shard_map/ppermute | solution.py:419
  61.7 36.7 %slice-start = ((f32[32,520,64]{1,2,0:T(8,128)}), f32[32,1,64]{1,2,0:T(8,128)S(1)}, s32[]{:S(2)}) async-start(f32[32,520,64]{1,2,0:T(8,128)} %all-gather.13.cloned.1.call-done), calls=%async_computation.9 | async-start | bytes 2097152 | tf_op jit(solution)/shard_map/slice | solution.py:376
  63.2 69.9 %copy-start.1 = (f32[8,512,64]{1,2,0:T(8,128)}, f32[8,512,64]{1,2,0:T(8,128)S(1)}, u32[]{:S(2)}) copy-start(f32[8,512,64]{1,2,0:T(8,128)S(1)} %slice.102) | copy-start | bytes 3145732
  78.9 20.4 %copy-start.2 = (f32[32,32,256]{2,1,0:T(8,128)}, f32[32,32,256]{2,1,0:T(8,128)S(1)}, u32[]{:S(2)}) copy-start(f32[32,32,256]{2,1,0:T(8,128)S(1)} %collective-permute-done.refs_2_) | copy-start | bytes 3145732
  78.9 20.3 %collective-permute-start.5 = (f32[32,32,256]{2,1,0:T(8,128)}, f32[32,32,256]{2,1,0:T(8,128)}, u32[]{:S(2)}, u32[]{:S(2)}) collective-permute-start(f32[32,32,256]{2,1,0:T(8,128)} %get-tuple-element.57), channel_id=1, source_target_pairs={{0,6},{8,14},{16,22},{24,30},{32,38},{40,46},{48,54},{56,62},{64,7... | collective-permute-start | bytes 3145736 | tf_op jit(solution)/shard_map/ppermute | solution.py:419
  80.5 18.7 %collective-permute-start.6 = (f32[32,32,256]{2,1,0:T(8,128)}, f32[32,32,256]{2,1,0:T(8,128)}, u32[]{:S(2)}, u32[]{:S(2)}) collective-permute-start(f32[32,32,256]{2,1,0:T(8,128)} %get-tuple-element.58), channel_id=1, source_target_pairs={{0,7},{8,15},{16,23},{24,31},{32,39},{40,47},{48,55},{56,63},{64,7... | collective-permute-start | bytes 3145736 | tf_op jit(solution)/shard_map/ppermute | solution.py:419
  133.1 31.1 %all-to-all-start.1 = ((f32[64,32,256]{2,1,0:T(8,128)}), f32[64,32,256]{2,1,0:T(8,128)S(1)}, u32[]{:S(2)}, u32[]{:S(2)}) async-start(f32[64,32,256]{2,1,0:T(8,128)} %slot_strips.1), calls=%async_computation.1 | async-start | bytes 4194304 | tf_op jit(solution)/shard_map/all_to_all | solution.py:415
  164.2 42.8 %all-to-all-start.2 = ((f32[64,2,32,256]{3,2,1,0:T(8,128)}), f32[64,2,32,256]{3,2,1,0:T(8,128)}, u32[]{:S(2)}, u32[]{:S(2)}) async-start(f32[64,2,32,256]{3,2,1,0:T(8,128)} %get-tuple-element.67), calls=%async_computation.2 | async-start | bytes 8388608 | tf_op jit(solution)/shard_map/all_to_all | solution.py:415
  170.9 72.5 %all-gather.9.cloned.1.call-start = ((), (), s32[]{:S(2)}) async-start(), calls=%async_computation.6 | async-start | bytes 5898240 | tf_op jit(solution)/shard_map/all_gather | solution.py:430
  193.5 24.2 %copy-start.3 = (pred[128,128]{0,1:T(8,128)(4,1)S(1)}, pred[128,128]{0,1:T(8,128)(4,1)}, u32[]{:S(2)}) copy-start(pred[128,128]{0,1:T(8,128)(4,1)} %copy.184) | copy-start | bytes 49156
  207.0 75.4 %all-to-all-start.3 = ((f32[64,3,32,256]{3,2,1,0:T(8,128)}), f32[64,3,32,256]{3,2,1,0:T(8,128)}, u32[]{:S(2)}, u32[]{:S(2)}) async-start(f32[64,3,32,256]{3,2,1,0:T(8,128)} %get-tuple-element.68), calls=%async_computation.3 | async-start | bytes 12582912 | tf_op jit(solution)/shard_map/all_to_all | solution.py:415
  247.0 45.6 %copy-start.7 = (s32[1,2,40]{2,1,0:T(2,128)S(1)}, s32[1,2,40]{2,1,0:T(2,128)}, u32[]{:S(2)}) copy-start(s32[1,2,40]{2,1,0:T(2,128)} %param.20) | copy-start | bytes 964
  247.0 45.9 %copy-start.9 = (s32[64]{0:T(128)S(1)}, s32[64]{0:T(128)}, u32[]{:S(2)}) copy-start(s32[64]{0:T(128)} %get-tuple-element.91) | copy-start | bytes 772
  282.4 187.0 %all-to-all-start.4 = ((f32[64,3,32,256]{3,2,1,0:T(8,128)}), f32[64,3,32,256]{3,2,1,0:T(8,128)}, u32[]{:S(2)}, u32[]{:S(2)}) async-start(f32[64,3,32,256]{3,2,1,0:T(8,128)} %get-tuple-element.69), calls=%async_computation.4 | async-start | bytes 12582912 | tf_op jit(solution)/shard_map/all_to_all | solution.py:415
  291.8 177.5 %all-reduce.7.cloned.1.call-start = ((), (), s32[]{:S(2)}) async-start(), calls=%async_computation.5 | async-start | bytes 5242880 | tf_op jit(solution)/shard_map/psum | solution.py:435
  (3 other events, 25.0 us)
Sparse Core Ops, SparseCore 0:
  11.2 50.4 all-gather.12
  63.4 44.1 all-gather.10
  175.3 67.9 all-gather.8
  294.7 174.5 all-reduce.6
